TPU v7x, 512 devices: a whole 4x8x8 slice. The times are simulated.
512 devices in a mesh: seg: 16 (over y, x_hi), grp: 32 (over z, x_lo, core).
Axes of the slice: x: 4 (x_hi: 2, x_lo: 2; x = x_hi * 2 + x_lo), y: 8, z: 8, core: 2. Of those that a mesh axis runs over, the one named last changes fastest.
Arguments:
- queries: bfloat16 [20480, 2048], P(('seg', 'grp')), may hold values from -8 to 8
- keys: bfloat16 [20480, 2048], P(('seg', 'grp')), may hold values from -8 to 8
- values: bfloat16 [20480, 2048], P(('seg', 'grp')), may hold values from -6 to 6
- rates: bfloat16 [20480, 32], P(('seg', 'grp')), may hold values from 0 to 0.45
- text_valid: int32 [16], P('seg'), may hold values from 32 to 128, as said below
- state_fwd: float32 [32, 64, 64], P('grp'), may hold values from -0.75 to 0.75
- state_bwd: float32 [32, 64, 64], P('grp'), may hold values from -0.75 to 0.75
Outputs:
- mixed: bfloat16 [20480, 2048], P(('seg', 'grp'))
Inputs may be any that keep to these rules, and one draw needn't show every extreme that they name: `text_valid`: the number of valid text tokens among the first 128 positions of each segment.
All inputs are finite; a program needn't handle non-finite values.
Results may differ from a plain program's by a relative error of at most 0.0045.
Values may be sent and summed in bfloat16 or wider, within the bound.
No kernel may reach another device: no remote copies, remote signals or barrier semaphores. Data moves between devices by JAX's collectives and lax.ppermute only.
A program may use at most 64 MiB of HBM per device.

v0:
```python
import functools
import math

import jax
import jax.numpy as jnp
from jax import lax
from jax.experimental import pallas as pl
from jax.experimental.pallas import tpu as pltpu
from jax.sharding import PartitionSpec as P

GROUP = 64
TEXT = 128
HDIM = 64
LANES = 128
QROWS = 256
VMEM_LIMIT = 48 * 1024 * 1024

bf16 = jnp.bfloat16
f32 = jnp.float32


def split(x):
    hi = x.astype(bf16)
    return hi, (x - hi.astype(f32)).astype(bf16)


def mm(a, b):
    return lax.dot_general(a, b, (((1,), (0,)), ((), ())), preferred_element_type=f32)


def mm_nt(a, b):
    return lax.dot_general(a, b, (((1,), (1,)), ((), ())), preferred_element_type=f32)


def mm_tn(a, b):
    return lax.dot_general(a, b, (((0,), (0,)), ((), ())), preferred_element_type=f32)


def mm3(a, b):
    a_hi, a_lo = split(a)
    b_hi, b_lo = split(b)
    return mm(jnp.concatenate([a_hi, a_lo, a_hi], axis=1), jnp.concatenate([b_hi, b_hi, b_lo], axis=0))


def lanes_left(rows):
    return lax.broadcasted_iota(jnp.int32, (rows, LANES), 1) < HDIM


def swap_halves(x):
    return pltpu.roll(x, HDIM, 1)


def pack_body(q_ref, k_ref, v_ref, r_ref, o_ref, rate_scr):
    rows, width = q_ref.shape
    heads = width // HDIM
    late = rows - 24
    left = lanes_left(rows)
    left24 = lanes_left(24)
    rate_scr[...] = jnp.zeros_like(rate_scr)
    rate_scr[:, 0:rows] = r_ref[...].astype(f32)
    for p in range(heads // 2):
        cols = slice(LANES * p, LANES * (p + 1))
        q = q_ref[:, cols].astype(f32)
        k = k_ref[:, cols].astype(f32)
        v = v_ref[:, cols].astype(f32)
        q_sw, k_sw, v_sw = swap_halves(q), swap_halves(k), swap_halves(v)
        for odd in (0, 1):
            head = 2 * p + odd
            qk = jnp.where(left, q_sw, k) if odd else jnp.where(left, q, k_sw)
            v_right, v_left = (v, v_sw) if odd else (v_sw, v)
            rate = jnp.broadcast_to(rate_scr[head : head + 1, :], (24 - late, LANES))
            low = jnp.concatenate([v_left[24:rows], rate], axis=0)
            vr = jnp.where(left24, low, v_right[0:24])
            o_ref[head] = jnp.concatenate([qk, vr], axis=0).astype(bf16)


def pack(queries, keys, values, rates_t):
    rows, width = queries.shape
    heads = width // HDIM
    return pl.pallas_call(
        pack_body,
        out_shape=jax.ShapeDtypeStruct((heads, rows + 24, LANES), bf16),
        scratch_shapes=[pltpu.VMEM((heads, LANES), f32)],
        compiler_params=pltpu.CompilerParams(vmem_limit_bytes=VMEM_LIMIT),
        name="pack",
    )(queries, keys, values, rates_t)


def attend_body(
    tv_ref, me_ref, recv_ref, msg_ref, xf_ref, xb_ref, kq_ref, yhi_ref, ylo_ref, att_ref, sq_ref,
    qk_scr, v_scr, r_scr,
):
    groups, rows, _ = recv_ref.shape
    toks = rows - 24
    late = toks - 24
    seglen = groups * toks
    chunks = seglen // GROUP
    valid = tv_ref[0]
    me = me_ref[0]

    pick = lax.broadcasted_iota(jnp.int32, (toks, LANES), 0) == lax.broadcasted_iota(jnp.int32, (toks, LANES), 1)
    for g in range(groups):
        block = recv_ref[g].astype(f32)
        base = toks * g
        qk_scr[base : base + toks] = block[0:toks]
        v_scr[base : base + 24] = block[toks : toks + 24]
        v_scr[base + 24 : base + toks] = swap_halves(block[toks : toks + late])
        r_scr[base : base + toks] = jnp.where(pick, block[toks + late : toks + late + 1], 0.0)

    v_all = v_scr[...].astype(bf16)
    kq_all = swap_halves(qk_scr[...]).astype(bf16)
    kq_ref[...] = kq_all

    row_id = lax.broadcasted_iota(jnp.int32, (2 * LANES, 2 * LANES), 0)
    col_id = lax.broadcasted_iota(jnp.int32, (2 * LANES, 2 * LANES), 1)
    is_key_row = lax.rem(row_id, LANES) >= HDIM
    sums = jnp.where(is_key_row == (col_id < LANES), 1.0, 0.0).astype(bf16)
    ones = jnp.ones((LANES, LANES), bf16)
    left = lanes_left(QROWS)
    cols = lax.broadcasted_iota(jnp.int32, (QROWS, TEXT), 1)

    for b in range(seglen // QROWS):
        at = slice(QROWS * b, QROWS * (b + 1))
        qk = qk_scr[at]
        squares_hi, squares_lo = split(qk * qk)
        total = mm(jnp.concatenate([squares_hi, squares_lo], axis=1), sums)
        inv = lax.rsqrt(total + 1e-06)
        inv_k = inv[:, 0:LANES]
        sq_ref[at] = math.sqrt(HDIM) * inv[:, LANES : 2 * LANES]
        rate = mm(r_scr[at].astype(bf16), ones)
        if QROWS * b < TEXT:
            position = QROWS * b + lax.broadcasted_iota(jnp.int32, (QROWS, LANES), 0)
            rate = jnp.where((position >= TEXT) | (position < valid), rate, 0.0)
        q_scaled = jnp.where(left, qk * (1.0 / math.sqrt(HDIM)), 0.0).astype(bf16)
        scores = mm_nt(q_scaled, kq_all)
        head_part = jnp.where(cols < valid, scores[:, 0:TEXT], -1e30)
        scores = jnp.concatenate([head_part, scores[:, TEXT:]], axis=1)
        peak = jnp.max(scores, axis=1, keepdims=True)
        raised = jnp.exp(scores - peak)
        row_total = jnp.sum(raised, axis=1, keepdims=True)
        gathered = mm(raised.astype(bf16), v_all)
        att = (gathered / row_total).astype(bf16)
        att_ref[at] = att
        step = rate * inv_k
        y = jnp.where(left, step * inv_k * swap_halves(qk), step * att.astype(f32))
        y_hi, y_lo = split(y)
        yhi_ref[at] = y_hi
        ylo_ref[at] = y_lo

    maps = []
    for n in range(chunks):
        at = slice(GROUP * n, GROUP * (n + 1))
        k = kq_ref[at, 0:HDIM]
        maps.append(mm_tn(jnp.concatenate([k, k], axis=0), jnp.concatenate([yhi_ref[at], ylo_ref[at]], axis=0)))

    left64 = lanes_left(HDIM)
    eye = jnp.where(
        lax.broadcasted_iota(jnp.int32, (HDIM, LANES), 0) == lax.broadcasted_iota(jnp.int32, (HDIM, LANES), 1), 1.0, 0.0
    )

    def advance(x, gb):
        return x - mm3(gb[:, 0:HDIM], x) + jnp.where(left64, 0.0, gb)

    forward, backward = eye, eye
    for n in range(chunks):
        xf_ref[n] = forward
        xb_ref[chunks - 1 - n] = backward
        forward = advance(forward, maps[n])
        backward = advance(backward, maps[chunks - 1 - n])
    forward = forward - eye
    backward = backward - eye
    for s in range(msg_ref.shape[0]):
        msg_ref[s] = jnp.where(s > me, forward, backward).astype(msg_ref.dtype)


def attend(text_valid, me, received, segments, link):
    groups, rows, _ = received.shape
    seglen = groups * (rows - 24)
    chunks = seglen // GROUP
    smem = pl.BlockSpec(memory_space=pltpu.SMEM)
    vmem = pl.BlockSpec(memory_space=pltpu.VMEM)
    tall = (seglen, LANES)
    return pl.pallas_call(
        attend_body,
        in_specs=[smem, smem, vmem],
        out_specs=[vmem] * 8,
        out_shape=[
            jax.ShapeDtypeStruct((segments, HDIM, LANES), link),
            jax.ShapeDtypeStruct((chunks, HDIM, LANES), f32),
            jax.ShapeDtypeStruct((chunks, HDIM, LANES), f32),
            jax.ShapeDtypeStruct(tall, bf16),
            jax.ShapeDtypeStruct(tall, bf16),
            jax.ShapeDtypeStruct(tall, bf16),
            jax.ShapeDtypeStruct(tall, bf16),
            jax.ShapeDtypeStruct(tall, f32),
        ],
        scratch_shapes=[pltpu.VMEM(tall, f32), pltpu.VMEM(tall, f32), pltpu.VMEM(tall, f32)],
        compiler_params=pltpu.CompilerParams(vmem_limit_bytes=VMEM_LIMIT),
        name="attend",
    )(text_valid, me, received)


def operators_body(xf_ref, xb_ref, kq_ref, yhi_ref, ylo_ref, att_ref, sq_ref, base_ref, ehi_ref, elo_ref):
    chunks = xf_ref.shape[0]
    row_id = lax.broadcasted_iota(jnp.int32, (GROUP, GROUP), 0)
    col_id = lax.broadcasted_iota(jnp.int32, (GROUP, GROUP), 1)
    left = lanes_left(GROUP)
    for n in range(chunks):
        at = slice(GROUP * n, GROUP * (n + 1))
        kq = kq_ref[at]
        q_first = swap_halves(kq.astype(f32))
        q = q_first[:, 0:HDIM]
        scores = mm_nt(q.astype(bf16), kq[:, 0:HDIM])
        both = jnp.concatenate(
            [jnp.where(col_id <= row_id, scores, 0.0), jnp.where(col_id >= row_id, scores, 0.0)], axis=0
        )
        both_hi, both_lo = split(both)
        y_hi, y_lo = yhi_ref[at], ylo_ref[at]
        pushed = mm(
            jnp.concatenate([both_hi, both_lo, both_hi], axis=1), jnp.concatenate([y_hi, y_hi, y_lo], axis=0)
        )
        scale = sq_ref[at]
        low, high = pushed[0:GROUP], pushed[GROUP : 2 * GROUP]
        op_f = (scale * (q_first - low))[:, 0:HDIM]
        op_b = (scale * (q_first - high))[:, 0:HDIM]
        from_f = mm3(op_f, xf_ref[n])
        from_b = mm3(op_b, xb_ref[n])
        base_ref[at] = att_ref[at].astype(f32) + scale * (low + high) + from_f + from_b
        reach = jnp.where(left, from_f, swap_halves(from_b))
        e_hi, e_lo = split(reach)
        ehi_ref[at] = e_hi
        elo_ref[at] = e_lo


def operators(xf, xb, kq, yhi, ylo, att, sq):
    tall = kq.shape
    return pl.pallas_call(
        operators_body,
        out_shape=[
            jax.ShapeDtypeStruct(tall, f32),
            jax.ShapeDtypeStruct(tall, bf16),
            jax.ShapeDtypeStruct(tall, bf16),
        ],
        compiler_params=pltpu.CompilerParams(vmem_limit_bytes=VMEM_LIMIT),
        cost_estimate=pl.CostEstimate(flops=2_000_000_000, bytes_accessed=8_000_000, transcendentals=0),
        name="operators",
    )(xf, xb, kq, yhi, ylo, att, sq)


def finish_body(me_ref, msg_ref, sf_ref, sb_ref, base_ref, ehi_ref, elo_ref, out_ref, scr):
    segments = msg_ref.shape[0]
    groups, half, _ = out_ref.shape
    me = me_ref[0]

    def follow(i, state):
        m = msg_ref[i].astype(f32)
        return state + mm3(m[:, 0:HDIM], state) + m[:, HDIM:LANES]

    w_f = lax.fori_loop(0, me, follow, sf_ref[0])
    w_b = lax.fori_loop(0, segments - 1 - me, lambda j, state: follow(segments - 1 - j, state), sb_ref[0])
    w = jnp.concatenate([w_f, w_b], axis=0)
    w_hi, w_lo = split(jnp.concatenate([w, w], axis=1))
    e_hi = ehi_ref[...]
    got = mm(jnp.concatenate([e_hi, elo_ref[...]], axis=1), jnp.concatenate([w_hi, w_hi], axis=0)) + mm(e_hi, w_lo)
    scr[...] = got + base_ref[...]
    left = lanes_left(half)
    for g in range(groups):
        first = scr[2 * half * g : 2 * half * g + half]
        second = scr[2 * half * g + half : 2 * half * (g + 1)]
        out_ref[g] = jnp.where(left, swap_halves(first), second).astype(bf16)


def finish(me, maps, state_fwd, state_bwd, base, ehi, elo, groups):
    seglen = base.shape[0]
    half = seglen // groups // 2
    smem = pl.BlockSpec(memory_space=pltpu.SMEM)
    vmem = pl.BlockSpec(memory_space=pltpu.VMEM)
    return pl.pallas_call(
        finish_body,
        in_specs=[smem] + [vmem] * 6,
        out_specs=vmem,
        out_shape=jax.ShapeDtypeStruct((groups, half, LANES), bf16),
        scratch_shapes=[pltpu.VMEM((seglen, LANES), f32)],
        compiler_params=pltpu.CompilerParams(vmem_limit_bytes=VMEM_LIMIT),
        name="finish",
    )(me, maps, state_fwd, state_bwd, base, ehi, elo)


def unpack_body(x_ref, out_ref, scr):
    heads, half, _ = x_ref.shape
    left = lanes_left(half)
    for p in range(heads // 2):
        even = x_ref[2 * p].astype(f32)
        odd = x_ref[2 * p + 1].astype(f32)
        scr[0:half] = jnp.where(left, even, swap_halves(odd))
        scr[half : 2 * half] = jnp.where(left, swap_halves(even), odd)
        out_ref[:, LANES * p : LANES * (p + 1)] = scr[...].astype(bf16)


def unpack(x):
    heads, half, _ = x.shape
    return pl.pallas_call(
        unpack_body,
        out_shape=jax.ShapeDtypeStruct((2 * half, heads * HDIM), bf16),
        scratch_shapes=[pltpu.VMEM((2 * half, LANES), f32)],
        compiler_params=pltpu.CompilerParams(vmem_limit_bytes=VMEM_LIMIT),
        name="unpack",
    )(x)


def exchange(x, axis):
    return lax.all_to_all(x, axis, split_axis=0, concat_axis=0, tiled=True)


def local(queries, keys, values, rates, text_valid, state_fwd, state_bwd):
    segments = lax.axis_size("seg")
    groups = lax.axis_size("grp")
    me = lax.axis_index("seg").astype(jnp.int32).reshape(1)
    received = exchange(pack(queries, keys, values, rates.T), "grp")
    msg, xf, xb, kq, yhi, ylo, att, sq = attend(text_valid, me, received, segments, f32)
    maps = exchange(msg, "seg")
    base, ehi, elo = operators(xf, xb, kq, yhi, ylo, att, sq)
    mixed = finish(me, maps, state_fwd, state_bwd, base, ehi, elo, groups)
    return unpack(exchange(mixed, "grp"))


def solution(mesh):
    in_specs = (
        P(("seg", "grp"), None),
        P(("seg", "grp"), None),
        P(("seg", "grp"), None),
        P(("seg", "grp"), None),
        P("seg"),
        P("grp", None, None),
        P("grp", None, None),
    )
    out_specs = P(("seg", "grp"), None)
    return jax.shard_map(local, mesh=mesh, in_specs=in_specs, out_specs=out_specs, check_vma=False)
```

profile of v0, /device:TPU:1, one launch (start us, length us, event | category | flops | bytes accessed | tf_op | source)
XLA Modules:
  0.0 92.2 jit_solution(11815931407259903962)
XLA Ops:
  0.0 0.0 copy-start
  0.0 0.9 copy-done
  0.9 0.0 copy-start.1
  0.9 0.9 copy-done.1
  1.8 0.0 copy-start.2
  1.8 0.9 copy-done.2
  2.7 0.0 copy-start.5
  2.8 0.7 copy-done.5
  3.4 1.0 %pack.1 = bf16[32,64,128]{2,1,0:T(8,128)(2,1)} custom-call(bf16[40,2048]{1,0:T(8,128)(2,1)S(1)} %copy-done, bf16[40,2048]{1,0:T(8,128)(2,1)S(1)} %copy-done.1, bf16[40,2048]{1,0:T(8,128)(2,1)S(1)} %copy-done.2, bf16[32,40]{1,0:T(8,128)(2,1)S(1)} %bitcast.2), custom_call_target="tpu_custom_call" | custom-call | tf_op jit(solution)/shard_map/pack/pallas_call | solution.py:80
  4.5 12.9 %all-to-all-start = ((bf16[32,64,128]{2,1,0:T(8,128)(2,1)}), bf16[32,64,128]{2,1,0:T(8,128)(2,1)S(1)}, u32[]{:S(2)}, u32[]{:S(2)}) async-start(bf16[32,64,128]{2,1,0:T(8,128)(2,1)} %pack.1), calls=%async_computation | async-start | bytes 1048576 | tf_op jit(solution)/shard_map/all_to_all | solution.py:312
  18.0 16.1 %all-to-all-done.recv_ref = bf16[32,64,128]{2,1,0:T(8,128)(2,1)S(1)} async-done(((bf16[32,64,128]{2,1,0:T(8,128)(2,1)}), bf16[32,64,128]{2,1,0:T(8,128)(2,1)S(1)}, u32[]{:S(2)}, u32[]{:S(2)}) %all-to-all-start) | async-done | bytes 524320 | tf_op jit(solution)/shard_map/all_to_all | solution.py:312
  34.1 8.1 %attend.1 = (f32[16,64,128]{2,1,0:T(8,128)}, f32[20,64,128]{2,1,0:T(8,128)S(1)}, f32[20,64,128]{2,1,0:T(8,128)S(1)}, bf16[1280,128]{1,0:T(8,128)(2,1)S(1)}, bf16...) custom-call(s32[1]{0:T(128)S(6)} %copy.8.tv_ref, ...), custom_call_target="tpu_custom_call" | custom-call | tf_op jit(solution)/shard_map/attend/pallas_call | solution.py:183
  42.2 0.0 copy-start.6
  42.2 0.8 copy-done.6
  43.1 0.0 copy-start.8
  43.1 0.7 copy-done.8
  43.8 0.0 copy-start.10
  43.8 0.0 copy-start.12
  43.8 0.7 copy-done.10
  44.5 0.1 copy-done.12
  44.6 9.1 %all-to-all-start.1 = ((f32[16,64,128]{2,1,0:T(8,128)}), f32[16,64,128]{2,1,0:T(8,128)S(1)}, u32[]{:S(2)}, u32[]{:S(2)}) async-start(f32[16,64,128]{2,1,0:T(8,128)} %get-tuple-element.16), calls=%async_computation.1 | async-start | bytes 1048576 | tf_op jit(solution)/shard_map/all_to_all | solution.py:312
  53.7 0.0 copy-start.7
  53.7 1.1 %copy-done.7 = f32[1280,128]{1,0:T(8,128)S(1)} copy-done((f32[1280,128]{1,0:T(8,128)S(1)}, f32[1280,128]{1,0:T(8,128)}, u32[]{:S(2)}) %copy-start.7) | copy-done | bytes 655384
  54.8 0.0 copy-start.9
  54.8 1.0 %copy-done.9 = bf16[1280,128]{1,0:T(8,128)(2,1)S(1)} copy-done((bf16[1280,128]{1,0:T(8,128)(2,1)S(1)}, bf16[1280,128]{1,0:T(8,128)(2,1)}, u32[]{:S(2)}) %copy-start.9) | copy-done | bytes 327704
  55.8 0.0 copy-start.11
  55.8 1.0 %copy-done.11 = bf16[1280,128]{1,0:T(8,128)(2,1)S(1)} copy-done((bf16[1280,128]{1,0:T(8,128)(2,1)S(1)}, bf16[1280,128]{1,0:T(8,128)(2,1)}, u32[]{:S(2)}) %copy-start.11) | copy-done | bytes 327704
  56.8 0.0 copy-start.13
  56.8 1.0 %copy-done.13 = bf16[1280,128]{1,0:T(8,128)(2,1)S(1)} copy-done((bf16[1280,128]{1,0:T(8,128)(2,1)S(1)}, bf16[1280,128]{1,0:T(8,128)(2,1)}, u32[]{:S(2)}) %copy-start.13) | copy-done | bytes 327704
  57.7 0.0 copy-start.3
  57.8 0.0 copy-start.4
  57.8 5.4 %operators.1 = (f32[1280,128]{1,0:T(8,128)S(1)}, bf16[1280,128]{1,0:T(8,128)(2,1)S(1)}, bf16[1280,128]{1,0:T(8,128)(2,1)S(1)}) custom-call(f32[20,64,128]{2,1,0:T(8,128)S(1)} %get-tuple-element.17.xf_ref, f32[20,64,128]{2,1,0:T(8,128)S(1)} %get-tuple-element.18.xb_ref, bf16[1280,128]{1,0:T(8,128)(2,1)S(1)} %get-tuple-element.19.kq_ref, ...), custom_call_target="tpu_custom_call" | custom-call | flops 2000000000 | bytes 8000000 | tf_op jit(solution)/shard_map/operators/pallas_call | solution.py:237
  63.2 7.0 %all-to-all-done.1.msg_ref = f32[16,64,128]{2,1,0:T(8,128)S(1)} async-done(((f32[16,64,128]{2,1,0:T(8,128)}), f32[16,64,128]{2,1,0:T(8,128)S(1)}, u32[]{:S(2)}, u32[]{:S(2)}) %all-to-all-start.1) | async-done | bytes 524320 | tf_op jit(solution)/shard_map/all_to_all | solution.py:312
  70.2 0.0 copy-done.3
  70.2 0.0 copy-done.4
  70.2 3.6 %finish.1 = bf16[32,20,128]{2,1,0:T(8,128)(2,1)S(1)} custom-call(s32[1]{0:T(128)} %bitcast.me_ref, f32[16,64,128]{2,1,0:T(8,128)S(1)} %all-to-all-done.1.msg_ref, f32[1,64,64]{2,1,0:T(8,128)S(1)} %copy-done.3, f32[1,64,64]{2,1,0:T(8,128)S(1)} %copy-done.4, f32[1280,128]{1,0:T(8,128)S(1)} %get-tuple-element.24.base_ref, ...), custom_call_target="tpu_custom_call" | custom-call | tf_op jit(solution)/shard_map/finish/pallas_call | solution.py:278
  73.8 17.6 %all_to_all.15.x_ref = bf16[32,20,128]{2,1,0:T(8,128)(2,1)S(1)} all-to-all(bf16[32,20,128]{2,1,0:T(8,128)(2,1)S(1)} %finish.1), channel_id=1, replica_groups=mesh['seg'=16,'grp'=32] {'grp'}, dimensions={0} | all-to-all | bytes 327680 | tf_op jit(solution)/shard_map/all_to_all | solution.py:312
  91.3 0.8 unpack.1
Async XLA Ops:
  0.0 0.9 copy-start
  0.9 0.9 copy-start.1
  1.8 0.9 copy-start.2
  2.7 0.7 copy-start.5
  4.5 29.6 %all-to-all-start = ((bf16[32,64,128]{2,1,0:T(8,128)(2,1)}), bf16[32,64,128]{2,1,0:T(8,128)(2,1)S(1)}, u32[]{:S(2)}, u32[]{:S(2)}) async-start(bf16[32,64,128]{2,1,0:T(8,128)(2,1)} %pack.1), calls=%async_computation | async-start | bytes 1048576 | tf_op jit(solution)/shard_map/all_to_all | solution.py:312
  42.2 0.9 copy-start.6
  43.1 0.7 copy-start.8
  43.8 0.7 copy-start.10
  43.8 0.8 copy-start.12
  44.6 25.6 %all-to-all-start.1 = ((f32[16,64,128]{2,1,0:T(8,128)}), f32[16,64,128]{2,1,0:T(8,128)S(1)}, u32[]{:S(2)}, u32[]{:S(2)}) async-start(f32[16,64,128]{2,1,0:T(8,128)} %get-tuple-element.16), calls=%async_computation.1 | async-start | bytes 1048576 | tf_op jit(solution)/shard_map/all_to_all | solution.py:312
  53.7 1.1 %copy-start.7 = (f32[1280,128]{1,0:T(8,128)S(1)}, f32[1280,128]{1,0:T(8,128)}, u32[]{:S(2)}) copy-start(f32[1280,128]{1,0:T(8,128)} %copy-done.6) | copy-start | bytes 1966084
  54.8 1.0 %copy-start.9 = (bf16[1280,128]{1,0:T(8,128)(2,1)S(1)}, bf16[1280,128]{1,0:T(8,128)(2,1)}, u32[]{:S(2)}) copy-start(bf16[1280,128]{1,0:T(8,128)(2,1)} %copy-done.8) | copy-start | bytes 983044
  55.8 1.0 %copy-start.11 = (bf16[1280,128]{1,0:T(8,128)(2,1)S(1)}, bf16[1280,128]{1,0:T(8,128)(2,1)}, u32[]{:S(2)}) copy-start(bf16[1280,128]{1,0:T(8,128)(2,1)} %copy-done.10) | copy-start | bytes 983044
  56.8 1.0 %copy-start.13 = (bf16[1280,128]{1,0:T(8,128)(2,1)S(1)}, bf16[1280,128]{1,0:T(8,128)(2,1)}, u32[]{:S(2)}) copy-start(bf16[1280,128]{1,0:T(8,128)(2,1)} %copy-done.12) | copy-start | bytes 983044
  57.7 12.4 %copy-start.3 = (f32[1,64,64]{2,1,0:T(8,128)S(1)}, f32[1,64,64]{2,1,0:T(8,128)}, u32[]{:S(2)}) copy-start(f32[1,64,64]{2,1,0:T(8,128)} %sf_ref.1) | copy-start | bytes 49156
  57.8 12.4 %copy-start.4 = (f32[1,64,64]{2,1,0:T(8,128)S(1)}, f32[1,64,64]{2,1,0:T(8,128)}, u32[]{:S(2)}) copy-start(f32[1,64,64]{2,1,0:T(8,128)} %sb_ref.1) | copy-start | bytes 49156
where the time goes:
time: 92.8 us; the launch traced here: 92.2 us
  waiting for transfers between devices  23.1 us (25%)
  starting transfers between devices  22 us (24%)
  Pallas kernels  19 us (20%)
  blocking collectives  17.6 us (19%)
  local copies, waits for them, and re-layouts  9.87 us (11%)
    all_to_all x2, waiting for transfers between devices, exchange(): return lax.all_to_all(x, axis, split_axis=0, concat_axis=0, tiled=True)  23.1 us
    all_to_all x2, starting transfers between devices, exchange(): return lax.all_to_all(x, axis, split_axis=0, concat_axis=0, tiled=True)  22 us
    all_to_all x1, blocking collectives, exchange(): return lax.all_to_all(x, axis, split_axis=0, concat_axis=0, tiled=True)  17.6 us
    unnamed x28, local copies, waits for them, and re-layouts  9.87 us
    pallas_call x1, Pallas kernels, attend(): pl.pallas_call(attend_body, in_specs=[smem, smem, vmem], out_specs=[vmem]...  8.12 us
    pallas_call x1, Pallas kernels, operators(): pl.pallas_call(operators_body, out_shape=[jax.ShapeDtypeStruct(tall, f32)...  5.45 us
    pallas_call x1, Pallas kernels, finish(): pl.pallas_call(finish_body, in_specs=[smem] + [vmem] * 6, out_specs=vmem,...  3.56 us
  transfers between devices with their start and end apart: 2, of which 2 were waited for; matrix products, arithmetic and copies ran while one was open for 0% of the time, Pallas kernels for 6%

commit v1 on v0

v1 whole, which is shorter than its diff:
```python
import math

import jax
import jax.numpy as jnp
from jax import lax
from jax.experimental import pallas as pl
from jax.experimental.pallas import tpu as pltpu
from jax.sharding import PartitionSpec as P

GROUP = 64
TEXT = 128
HDIM = 64
LANES = 128
QROWS = 256
VMEM_LIMIT = 24 * 1024 * 1024
PACK_LIMIT = 62 * 1024 * 1024

bf16 = jnp.bfloat16
f32 = jnp.float32


def split(x):
    hi = x.astype(bf16)
    return hi, (x - hi.astype(f32)).astype(bf16)


def mm(a, b):
    return lax.dot_general(a, b, (((1,), (0,)), ((), ())), preferred_element_type=f32)


def mm_nt(a, b):
    return lax.dot_general(a, b, (((1,), (1,)), ((), ())), preferred_element_type=f32)


def mm_tn(a, b):
    return lax.dot_general(a, b, (((0,), (0,)), ((), ())), preferred_element_type=f32)


def lanes_left(rows):
    return lax.broadcasted_iota(jnp.int32, (rows, LANES), 1) < HDIM


def swap_halves(x):
    return pltpu.roll(x, HDIM, 1)


def pack_body(q_hbm, k_hbm, v_hbm, r_hbm, o_ref, q_ref, k_ref, v_ref, r_ref, rate_scr, sems):
    copies = [
        pltpu.make_async_copy(source, target, sems.at[i])
        for i, (source, target) in enumerate(((r_hbm, r_ref), (q_hbm, q_ref), (k_hbm, k_ref), (v_hbm, v_ref)))
    ]
    for copy in copies:
        copy.start()
    rows, width = q_ref.shape
    heads = width // HDIM
    late = rows - 24
    left = lanes_left(rows)
    left24 = lanes_left(24)
    rate_scr[...] = jnp.zeros_like(rate_scr)
    for copy in copies:
        copy.wait()
    rate_scr[:, 0:rows] = r_ref[...].astype(f32)
    for p in range(heads // 2):
        cols = slice(LANES * p, LANES * (p + 1))
        q = q_ref[:, cols].astype(f32)
        k = k_ref[:, cols].astype(f32)
        v = v_ref[:, cols].astype(f32)
        q_sw, k_sw, v_sw = swap_halves(q), swap_halves(k), swap_halves(v)
        for odd in (0, 1):
            head = 2 * p + odd
            qk = jnp.where(left, q_sw, k) if odd else jnp.where(left, q, k_sw)
            v_right, v_left = (v, v_sw) if odd else (v_sw, v)
            rate = jnp.broadcast_to(rate_scr[head : head + 1, :], (24 - late, LANES))
            low = jnp.concatenate([v_left[24:rows], rate], axis=0)
            vr = jnp.where(left24, low, v_right[0:24])
            o_ref[head] = jnp.concatenate([qk, vr], axis=0).astype(bf16)


def pack(queries, keys, values, rates_t):
    rows, width = queries.shape
    heads = width // HDIM
    return pl.pallas_call(
        pack_body,
        in_specs=[pl.BlockSpec(memory_space=pl.ANY)] * 4,
        out_shape=jax.ShapeDtypeStruct((heads, rows + 24, LANES), bf16),
        scratch_shapes=[
            pltpu.VMEM((rows, width), bf16),
            pltpu.VMEM((rows, width), bf16),
            pltpu.VMEM((rows, width), bf16),
            pltpu.VMEM((heads, rows), bf16),
            pltpu.VMEM((heads, LANES), f32),
            pltpu.SemaphoreType.DMA((4,)),
        ],
        compiler_params=pltpu.CompilerParams(vmem_limit_bytes=PACK_LIMIT),
        name="pack",
    )(queries, keys, values, rates_t)


def packed(x):
    hi, lo = split(x)
    return jnp.where(lanes_left(x.shape[0]), hi.astype(f32), lo.astype(f32)).astype(bf16)


def twice(p):
    return jnp.concatenate([p, p], axis=1)


def four(hi, lo):
    return jnp.concatenate([hi, hi, lo, lo], axis=0)


def doubled_eye():
    row = lax.broadcasted_iota(jnp.int32, (HDIM, LANES), 0)
    col = lax.broadcasted_iota(jnp.int32, (HDIM, LANES), 1)
    return jnp.where(row == lax.rem(col, HDIM), 1.0, 0.0).astype(f32)


def attend_body(
    tv_ref, me_ref, recv_ref, msg_ref, q2_ref, k2_ref, ckh_ref, ckl_ref, dah_ref, dal_ref, att_ref, sq_ref, g_ref,
    qk_scr, v_scr, r_scr, qs_scr, step_scr, kf_scr, kb_scr,
):
    groups, rows, _ = recv_ref.shape
    toks = rows - 24
    late = toks - 24
    seglen = groups * toks
    chunks = seglen // GROUP
    blocks = seglen // QROWS
    valid = tv_ref[0]
    me = me_ref[0]

    pick = lax.broadcasted_iota(jnp.int32, (toks, LANES), 0) == lax.broadcasted_iota(jnp.int32, (toks, LANES), 1)
    left24, left_late = lanes_left(24), lanes_left(late)
    for g in range(groups):
        block = recv_ref[g].astype(f32)
        base = toks * g
        qk_scr[base : base + toks] = block[0:toks]
        tail = block[toks : toks + 24]
        tail_sw = swap_halves(tail)
        v_scr[base : base + 24] = jnp.where(left24, tail_sw, tail)
        v_scr[base + 24 : base + toks] = jnp.where(left_late, tail[0:late], tail_sw[0:late])
        r_scr[base : base + toks] = jnp.where(pick, tail[late : late + 1], 0.0)

    row_id = lax.broadcasted_iota(jnp.int32, (2 * LANES, 2 * LANES), 0)
    col_id = lax.broadcasted_iota(jnp.int32, (2 * LANES, 2 * LANES), 1)
    is_key_row = lax.rem(row_id, LANES) >= HDIM
    sums = jnp.where(is_key_row == (col_id < LANES), 1.0, 0.0).astype(bf16)
    ones = jnp.ones((LANES, LANES), bf16)
    left = lanes_left(QROWS)
    cols = lax.broadcasted_iota(jnp.int32, (QROWS, TEXT), 1)

    for b in range(blocks):
        at = slice(QROWS * b, QROWS * (b + 1))
        qk = qk_scr[at]
        kq = swap_halves(qk)
        k2 = jnp.where(left, kq, qk)
        k2_ref[at] = k2.astype(bf16)
        q2_ref[at] = jnp.where(left, qk, kq).astype(bf16)
        qs_scr[at] = jnp.where(left, qk * (1.0 / math.sqrt(HDIM)), 0.0).astype(bf16)
        squares_hi, squares_lo = split(qk * qk)
        inv = lax.rsqrt(mm(jnp.concatenate([squares_hi, squares_lo], axis=1), sums) + 1e-06)
        inv_k = inv[:, 0:LANES]
        sq_ref[at] = math.sqrt(HDIM) * inv[:, LANES : 2 * LANES]
        rate = mm(r_scr[at].astype(bf16), ones)
        if QROWS * b < TEXT:
            position = QROWS * b + lax.broadcasted_iota(jnp.int32, (QROWS, LANES), 0)
            rate = jnp.where((position >= TEXT) | (position < valid), rate, 0.0)
        step = rate * inv_k
        step_scr[at] = step
        ck_hi, ck_lo = split(step * inv_k * k2)
        ckh_ref[at] = ck_hi
        ckl_ref[at] = ck_lo

    for n in range(chunks):
        at = slice(GROUP * n, GROUP * (n + 1))
        k = k2_ref[at, 0:HDIM]
        gram = mm_tn(jnp.concatenate([k, k], axis=0), jnp.concatenate([ckh_ref[at], ckl_ref[at]], axis=0))
        g_hi, g_lo = split(gram)
        g_ref[n, 0:HDIM] = g_hi
        g_ref[n, HDIM : 2 * HDIM] = g_lo

    v2 = v_scr[...].astype(bf16)
    eye = doubled_eye()
    t_f, t_b = eye, eye

    def advance(t, n, keep_ref):
        at = slice(GROUP * n, GROUP * (n + 1))
        p = packed(t)
        keep_ref[at] = packed(mm_nt(k2_ref[at], jnp.concatenate([p, p], axis=0)))
        return t - mm(twice(p), four(g_ref[n, 0:HDIM], g_ref[n, HDIM : 2 * HDIM]))

    for b in range(blocks):
        at = slice(QROWS * b, QROWS * (b + 1))
        scores = mm_nt(qs_scr[at], k2_ref[...])
        for n in range(chunks * b // blocks, chunks * (b + 1) // blocks):
            t_f = advance(t_f, n, kf_scr)
            t_b = advance(t_b, chunks - 1 - n, kb_scr)
        head_part = jnp.where(cols < valid, scores[:, 0:TEXT], -1e30)
        scores = jnp.concatenate([head_part, scores[:, TEXT:]], axis=1)
        peak = jnp.max(scores, axis=1, keepdims=True)
        raised = jnp.exp(scores - peak)
        row_total = jnp.sum(raised, axis=1, keepdims=True)
        gathered = mm(raised.astype(bf16), v2)
        att = (gathered / row_total).astype(bf16)
        att_ref[at] = att
        da_hi, da_lo = split(step_scr[at] * att.astype(f32))
        dah_ref[at] = da_hi
        dal_ref[at] = da_lo

    total = jnp.zeros((LANES, 2 * LANES), f32)
    for b in range(blocks):
        at = slice(QROWS * b, QROWS * (b + 1))
        da = jnp.where(left, dah_ref[at].astype(f32), dal_ref[at].astype(f32)).astype(bf16)
        total = total + mm_tn(da, jnp.concatenate([kf_scr[at], kb_scr[at]], axis=1))
    total = total[0:HDIM] + total[HDIM : 2 * HDIM]
    from_f, from_b = total[:, 0:LANES], total[:, LANES : 2 * LANES]
    shift_b = from_f + swap_halves(from_f)
    shift_f = from_b + swap_halves(from_b)
    left64 = lanes_left(HDIM)
    later = jnp.where(left64, t_f - eye, shift_f)
    earlier = jnp.where(left64, t_b - eye, shift_b)
    for s in range(msg_ref.shape[0]):
        msg_ref[s] = jnp.where(s > me, later, earlier).astype(msg_ref.dtype)


def attend(text_valid, me, received, segments, link):
    groups, rows, _ = received.shape
    seglen = groups * (rows - 24)
    chunks = seglen // GROUP
    smem = pl.BlockSpec(memory_space=pltpu.SMEM)
    vmem = pl.BlockSpec(memory_space=pltpu.VMEM)
    tall = (seglen, LANES)
    return pl.pallas_call(
        attend_body,
        in_specs=[smem, smem, vmem],
        out_specs=[vmem] * 10,
        out_shape=[jax.ShapeDtypeStruct((segments, HDIM, LANES), link)]
        + [jax.ShapeDtypeStruct(tall, bf16)] * 7
        + [jax.ShapeDtypeStruct(tall, f32), jax.ShapeDtypeStruct((chunks, LANES, LANES), bf16)],
        scratch_shapes=[
            pltpu.VMEM(tall, f32), pltpu.VMEM(tall, f32), pltpu.VMEM(tall, f32), pltpu.VMEM(tall, bf16),
            pltpu.VMEM(tall, f32), pltpu.VMEM(tall, bf16), pltpu.VMEM(tall, bf16),
        ],
        compiler_params=pltpu.CompilerParams(vmem_limit_bytes=VMEM_LIMIT),
        name="attend",
    )(text_valid, me, received)


def operators_body(
    q2_ref, k2_ref, ckh_ref, ckl_ref, dah_ref, dal_ref, att_ref, sq_ref, g_ref, base_ref, ehi_ref, elo_ref,
    opf_scr, opb_scr, xf_scr, xb_scr,
):
    chunks = g_ref.shape[0]
    row_id = lax.broadcasted_iota(jnp.int32, (GROUP, LANES), 0)
    col_id = lax.rem(lax.broadcasted_iota(jnp.int32, (GROUP, LANES), 1), GROUP)
    left = lanes_left(GROUP)
    eye = doubled_eye()
    x_f = jnp.concatenate([eye, jnp.zeros_like(eye)], axis=0)
    x_b = x_f

    def rows_of(n):
        return slice(GROUP * n, GROUP * (n + 1))

    def advance(x, n, keep_ref):
        at = rows_of(n)
        hi, lo = split(x)
        keep_ref[n] = jnp.concatenate([hi, lo], axis=1)
        p = jnp.where(lanes_left(2 * HDIM), hi.astype(f32), lo.astype(f32)).astype(bf16)
        k2 = k2_ref[at]
        pushed = mm_tn(
            jnp.concatenate([dah_ref[at, 0:HDIM], dal_ref[at, 0:HDIM]], axis=0), jnp.concatenate([k2, k2], axis=0)
        )
        x = x - mm(twice(p), four(g_ref[n, 0:HDIM], g_ref[n, HDIM : 2 * HDIM]))
        return jnp.concatenate([x[0:HDIM], x[HDIM : 2 * HDIM] + pushed], axis=0)

    for n in range(chunks):
        x_f = advance(x_f, n, xf_scr)
        x_b = advance(x_b, chunks - 1 - n, xb_scr)
        at = rows_of(n)
        k2, q2 = k2_ref[at], q2_ref[at]
        scores = mm_nt(q2[:, 0:HDIM], jnp.concatenate([k2, k2], axis=0)[:, 0:HDIM])
        both = packed(
            jnp.concatenate(
                [jnp.where(col_id <= row_id, scores, 0.0), jnp.where(col_id >= row_id, scores, 0.0)], axis=0
            )
        )
        y_hi = jnp.concatenate([ckh_ref[at], dah_ref[at]], axis=1)
        y_lo = jnp.concatenate([ckl_ref[at], dal_ref[at]], axis=1)
        pushed = mm(twice(both), four(y_hi, y_lo))
        scale = sq_ref[at]
        q = q2.astype(f32)
        opf_scr[at] = packed(scale * (q - pushed[0:GROUP, 0:LANES]))
        opb_scr[at] = packed(scale * (q - pushed[GROUP : 2 * GROUP, 0:LANES]))
        base_ref[at] = att_ref[at].astype(f32) + scale * (
            pushed[0:GROUP, LANES : 2 * LANES] + pushed[GROUP : 2 * GROUP, LANES : 2 * LANES]
        )

    for n in range(chunks):
        at = rows_of(n)

        def through(op_ref, x_ref):
            t, w = x_ref[n, 0:HDIM], x_ref[n, HDIM : 2 * HDIM]
            return mm_nt(twice(op_ref[at]), jnp.concatenate([t, t, w, w], axis=0))

        from_f, from_b = through(opf_scr, xf_scr), through(opb_scr, xb_scr)
        base_ref[at] = base_ref[at] + from_f[:, LANES : 2 * LANES] + from_b[:, LANES : 2 * LANES]
        e_hi, e_lo = split(jnp.where(left, from_f[:, 0:LANES], from_b[:, 0:LANES]))
        ehi_ref[at] = e_hi
        elo_ref[at] = e_lo


def operators(*held):
    tall = held[0].shape
    chunks = tall[0] // GROUP
    state = (chunks, 2 * HDIM, 2 * LANES)
    return pl.pallas_call(
        operators_body,
        out_shape=[
            jax.ShapeDtypeStruct(tall, f32),
            jax.ShapeDtypeStruct(tall, bf16),
            jax.ShapeDtypeStruct(tall, bf16),
        ],
        scratch_shapes=[
            pltpu.VMEM(tall, bf16), pltpu.VMEM(tall, bf16), pltpu.VMEM(state, bf16), pltpu.VMEM(state, bf16),
        ],
        compiler_params=pltpu.CompilerParams(vmem_limit_bytes=VMEM_LIMIT),
        cost_estimate=pl.CostEstimate(flops=2_000_000_000, bytes_accessed=8_000_000, transcendentals=0),
        name="operators",
    )(*held)


def finish_body(me_ref, msg_ref, sf_ref, sb_ref, base_ref, ehi_ref, elo_ref, out_ref, scr):
    segments = msg_ref.shape[0]
    groups, half, _ = out_ref.shape
    me = me_ref[0]
    left64 = lanes_left(HDIM)

    def doubled_transpose(state):
        return jnp.concatenate([state, state], axis=0).T

    def follow(i, live, state):
        m = jnp.where(live, msg_ref[i].astype(f32), 0.0)
        m_sw = swap_halves(m)
        decay = jnp.where(left64, m, m_sw)
        shift = jnp.where(left64, m_sw, m)
        hi, lo = split(decay)
        return state + mm(twice(packed(state)), four(hi, lo)) + shift

    w_f, w_b = doubled_transpose(sf_ref[0]), doubled_transpose(sb_ref[0])
    for i in range(segments - 1):
        w_f = follow(i, i < me, w_f)
        w_b = follow(segments - 1 - i, segments - 1 - i > me, w_b)
    w_hi, w_lo = split(jnp.where(left64, w_f, w_b))
    w_row = jnp.concatenate([w_hi, w_hi, w_lo], axis=1)
    e_hi = ehi_ref[...]
    got = mm_nt(jnp.concatenate([e_hi, elo_ref[...], e_hi], axis=1), jnp.concatenate([w_row, w_row], axis=0))
    scr[...] = got + base_ref[...]
    left = lanes_left(half)
    for g in range(groups):
        first = scr[2 * half * g : 2 * half * g + half]
        second = scr[2 * half * g + half : 2 * half * (g + 1)]
        out_ref[g] = jnp.where(left, first, second).astype(bf16)


def finish(me, maps, state_fwd, state_bwd, base, ehi, elo, groups):
    seglen = base.shape[0]
    half = seglen // groups // 2
    smem = pl.BlockSpec(memory_space=pltpu.SMEM)
    vmem = pl.BlockSpec(memory_space=pltpu.VMEM)
    return pl.pallas_call(
        finish_body,
        in_specs=[smem] + [vmem] * 6,
        out_specs=vmem,
        out_shape=jax.ShapeDtypeStruct((groups, half, LANES), bf16),
        scratch_shapes=[pltpu.VMEM((seglen, LANES), f32)],
        compiler_params=pltpu.CompilerParams(vmem_limit_bytes=VMEM_LIMIT),
        name="finish",
    )(me, maps, state_fwd, state_bwd, base, ehi, elo)


def unpack_body(x_ref, out_ref, scr):
    heads, half, _ = x_ref.shape
    left = lanes_left(half)
    for p in range(heads // 2):
        even = x_ref[2 * p].astype(f32)
        odd = x_ref[2 * p + 1].astype(f32)
        scr[0:half] = jnp.where(left, even, swap_halves(odd))
        scr[half : 2 * half] = jnp.where(left, swap_halves(even), odd)
        out_ref[:, LANES * p : LANES * (p + 1)] = scr[...].astype(bf16)


def unpack(x):
    heads, half, _ = x.shape
    return pl.pallas_call(
        unpack_body,
        out_shape=jax.ShapeDtypeStruct((2 * half, heads * HDIM), bf16),
        scratch_shapes=[pltpu.VMEM((2 * half, LANES), f32)],
        compiler_params=pltpu.CompilerParams(vmem_limit_bytes=VMEM_LIMIT),
        name="unpack",
    )(x)


def exchange(x, axis):
    return lax.all_to_all(x, axis, split_axis=0, concat_axis=0, tiled=True)


def local(queries, keys, values, rates, text_valid, state_fwd, state_bwd):
    segments = lax.axis_size("seg")
    groups = lax.axis_size("grp")
    me = lax.axis_index("seg").astype(jnp.int32).reshape(1)
    received = exchange(pack(queries, keys, values, rates.T), "grp")
    msg, *held = attend(text_valid, me, received, segments, bf16)
    maps = exchange(msg, "seg")
    base, ehi, elo = operators(*held)
    mixed = finish(me, maps, state_fwd, state_bwd, base, ehi, elo, groups)
    return unpack(exchange(mixed, "grp"))


def solution(mesh):
    in_specs = (
        P(("seg", "grp"), None),
        P(("seg", "grp"), None),
        P(("seg", "grp"), None),
        P(("seg", "grp"), None),
        P("seg"),
        P("grp", None, None),
        P("grp", None, None),
    )
    out_specs = P(("seg", "grp"), None)
    return jax.shard_map(local, mesh=mesh, in_specs=in_specs, out_specs=out_specs, check_vma=False)
```

time: 92.8 us -> 82.9 us (0.89)
  waiting for transfers between devices: 23.1 us -> 17.1 us
  Pallas kernels: 19 us -> 15.9 us
    all_to_all x2, waiting for transfers between devices: 23.1 us -> 17.1 us  [exchange(): return lax.all_to_all(x, axis, split_axis=0, concat_axis=0, tiled=True)]
    pallas_call x1, Pallas kernels: 8.12 us -> 6.09 us  [attend(): pl.pallas_call(attend_body, in_specs=[smem, smem, vmem], out_specs=[vmem]...]
    pallas_call x1, Pallas kernels: 1.02 us -> 2.12 us  [pack(): pl.pallas_call(pack_body, in_specs=[pl.BlockSpec(memory_space=pl.ANY)] *...]
    pallas_call x1, Pallas kernels: 5.45 us -> 4.35 us  [operators(): pl.pallas_call(operators_body, out_shape=[jax.ShapeDtypeStruct(tall, f32)...]
    pallas_call x1, Pallas kernels: 3.56 us -> 2.53 us  [finish(): pl.pallas_call(finish_body, in_specs=[smem] + [vmem] * 6, out_specs=vmem,...]
  transfers between devices with their start and end apart: 2 -> 2, of which waited for: 2 -> 2; matrix products, arithmetic and copies ran while one was open for 0% -> 0% of each run, Pallas kernels for 6% -> 5%
where the time goes in v1:
time: 82.9 us; the launch traced here: 82.3 us
  starting transfers between devices  22 us (27%)
  waiting for transfers between devices  17.1 us (21%)
  blocking collectives  17.1 us (21%)
  Pallas kernels  15.9 us (19%)
  local copies, waits for them, and re-layouts  9.48 us (11%)
    all_to_all x2, starting transfers between devices, exchange(): return lax.all_to_all(x, axis, split_axis=0, concat_axis=0, tiled=True)  22 us
    all_to_all x2, waiting for transfers between devices, exchange(): return lax.all_to_all(x, axis, split_axis=0, concat_axis=0, tiled=True)  17.1 us
    all_to_all x1, blocking collectives, exchange(): return lax.all_to_all(x, axis, split_axis=0, concat_axis=0, tiled=True)  17.1 us
    unnamed x28, local copies, waits for them, and re-layouts  9.48 us
    pallas_call x1, Pallas kernels, attend(): pl.pallas_call(attend_body, in_specs=[smem, smem, vmem], out_specs=[vmem]...  6.09 us
    pallas_call x1, Pallas kernels, operators(): pl.pallas_call(operators_body, out_shape=[jax.ShapeDtypeStruct(tall, f32)...  4.35 us
    pallas_call x1, Pallas kernels, finish(): pl.pallas_call(finish_body, in_specs=[smem] + [vmem] * 6, out_specs=vmem,...  2.53 us
    pallas_call x1, Pallas kernels, pack(): pl.pallas_call(pack_body, in_specs=[pl.BlockSpec(memory_space=pl.ANY)] *...  2.12 us
  transfers between devices with their start and end apart: 2, of which 2 were waited for; matrix products, arithmetic and copies ran while one was open for 0% of the time, Pallas kernels for 5%

profile of v1, /device:TPU:1, one launch (start us, length us, event | category | flops | bytes accessed | tf_op | source)
XLA Modules:
  0.0 82.3 jit_solution(5968729883723933248)
XLA Ops:
  0.0 2.1 %pack.1 = bf16[32,64,128]{2,1,0:T(8,128)(2,1)} custom-call(bf16[40,2048]{1,0:T(8,128)(2,1)} %q_hbm.1, bf16[40,2048]{1,0:T(8,128)(2,1)} %k_hbm.1, bf16[40,2048]{1,0:T(8,128)(2,1)} %v_hbm.1, bf16[32,40]{1,0:T(8,128)(2,1)} %bitcast.2), custom_call_target="tpu_custom_call" | custom-call | tf_op jit(solution)/shard_map/pack/pallas_call | solution.py:82
  2.1 12.9 %all-to-all-start = ((bf16[32,64,128]{2,1,0:T(8,128)(2,1)}), bf16[32,64,128]{2,1,0:T(8,128)(2,1)S(1)}, u32[]{:S(2)}, u32[]{:S(2)}) async-start(bf16[32,64,128]{2,1,0:T(8,128)(2,1)} %pack.1), calls=%async_computation | async-start | bytes 1048576 | tf_op jit(solution)/shard_map/all_to_all | solution.py:403
  15.7 16.1 %all-to-all-done.recv_ref = bf16[32,64,128]{2,1,0:T(8,128)(2,1)S(1)} async-done(((bf16[32,64,128]{2,1,0:T(8,128)(2,1)}), bf16[32,64,128]{2,1,0:T(8,128)(2,1)S(1)}, u32[]{:S(2)}, u32[]{:S(2)}) %all-to-all-start) | async-done | bytes 524320 | tf_op jit(solution)/shard_map/all_to_all | solution.py:403
  31.8 6.1 %attend.1 = (bf16[16,64,128]{2,1,0:T(8,128)(2,1)}, bf16[1280,128]{1,0:T(8,128)(2,1)S(1)}, bf16[1280,128]{1,0:T(8,128)(2,1)S(1)}, bf16[1280,128]{1,0:T(8,128)(2,1...) custom-call(s32[1]{0:T(128)S(6)} %copy.8.tv_ref, ...), custom_call_target="tpu_custom_call" | custom-call | tf_op jit(solution)/shard_map/attend/pallas_call | solution.py:232
  37.9 0.0 copy-start.2
  37.9 0.7 copy-done.2
  38.6 0.0 copy-start.4
  38.6 0.7 copy-done.4
  39.3 0.0 copy-start.6
  39.3 0.7 copy-done.6
  40.0 0.0 copy-start.8
  40.0 0.7 copy-done.8
  40.8 0.0 copy-start.10
  40.8 0.7 copy-done.10
  41.5 0.0 copy-start.12
  41.5 9.1 %all-to-all-start.1 = ((bf16[16,64,128]{2,1,0:T(8,128)(2,1)}), bf16[16,64,128]{2,1,0:T(8,128)(2,1)S(1)}, u32[]{:S(2)}, u32[]{:S(2)}) async-start(bf16[16,64,128]{2,1,0:T(8,128)(2,1)} %get-tuple-element.18), calls=%async_computation.1 | async-start | bytes 524288 | tf_op jit(solution)/shard_map/all_to_all | solution.py:403
  50.6 0.0 copy-done.12
  50.6 0.0 copy-start.3
  50.6 1.0 %copy-done.3 = bf16[1280,128]{1,0:T(8,128)(2,1)S(1)} copy-done((bf16[1280,128]{1,0:T(8,128)(2,1)S(1)}, bf16[1280,128]{1,0:T(8,128)(2,1)}, u32[]{:S(2)}) %copy-start.3) | copy-done | bytes 327704
  51.6 0.0 copy-start.5
  51.6 1.0 %copy-done.5 = bf16[1280,128]{1,0:T(8,128)(2,1)S(1)} copy-done((bf16[1280,128]{1,0:T(8,128)(2,1)S(1)}, bf16[1280,128]{1,0:T(8,128)(2,1)}, u32[]{:S(2)}) %copy-start.5) | copy-done | bytes 327704
  52.6 0.0 copy-start.7
  52.6 1.0 %copy-done.7 = bf16[1280,128]{1,0:T(8,128)(2,1)S(1)} copy-done((bf16[1280,128]{1,0:T(8,128)(2,1)S(1)}, bf16[1280,128]{1,0:T(8,128)(2,1)}, u32[]{:S(2)}) %copy-start.7) | copy-done | bytes 327704
  53.5 0.0 copy-start.9
  53.5 1.0 %copy-done.9 = bf16[1280,128]{1,0:T(8,128)(2,1)S(1)} copy-done((bf16[1280,128]{1,0:T(8,128)(2,1)S(1)}, bf16[1280,128]{1,0:T(8,128)(2,1)}, u32[]{:S(2)}) %copy-start.9) | copy-done | bytes 327704
  54.5 0.0 copy-start.11
  54.5 1.0 %copy-done.11 = bf16[1280,128]{1,0:T(8,128)(2,1)S(1)} copy-done((bf16[1280,128]{1,0:T(8,128)(2,1)S(1)}, bf16[1280,128]{1,0:T(8,128)(2,1)}, u32[]{:S(2)}) %copy-start.11) | copy-done | bytes 327704
  55.5 0.0 copy-start.13
  55.5 1.0 %copy-done.13 = bf16[1280,128]{1,0:T(8,128)(2,1)S(1)} copy-done((bf16[1280,128]{1,0:T(8,128)(2,1)S(1)}, bf16[1280,128]{1,0:T(8,128)(2,1)}, u32[]{:S(2)}) %copy-start.13) | copy-done | bytes 327704
  56.5 0.0 copy-start
  56.5 0.0 copy-start.1
  56.5 4.3 %operators.1 = (f32[1280,128]{1,0:T(8,128)S(1)}, bf16[1280,128]{1,0:T(8,128)(2,1)S(1)}, bf16[1280,128]{1,0:T(8,128)(2,1)S(1)}) custom-call(bf16[1280,128]{1,0:T(8,128)(2,1)S(1)} %get-tuple-element.19.q2_ref, bf16[1280,128]{1,0:T(8,128)(2,1)S(1)} %copy-done.3, bf16[1280,128]{1,0:T(8,128)(2,1)S(1)} %copy-done.5, bf16[1280,128]{1,0:T(8,128)(2,1)S(1)} %copy-done.7, ...), custom_call_target="tpu_custom_call" | custom-call | flops 2000000000 | bytes 8000000 | tf_op jit(solution)/shard_map/operators/pallas_call | solution.py:315
  60.8 1.0 %all-to-all-done.1.msg_ref = bf16[16,64,128]{2,1,0:T(8,128)(2,1)S(1)} async-done(((bf16[16,64,128]{2,1,0:T(8,128)(2,1)}), bf16[16,64,128]{2,1,0:T(8,128)(2,1)S(1)}, u32[]{:S(2)}, u32[]{:S(2)}) %all-to-all-start.1) | async-done | bytes 262176 | tf_op jit(solution)/shard_map/all_to_all | solution.py:403
  61.9 0.0 copy-done
  61.9 0.0 copy-done.1
  61.9 2.5 %finish.1 = bf16[32,20,128]{2,1,0:T(8,128)(2,1)S(1)} custom-call(s32[1]{0:T(128)} %bitcast.me_ref, bf16[16,64,128]{2,1,0:T(8,128)(2,1)S(1)} %all-to-all-done.1.msg_ref, f32[1,64,64]{2,1,0:T(8,128)S(1)} %copy-done, f32[1,64,64]{2,1,0:T(8,128)S(1)} %copy-done.1, f32[1280,128]{1,0:T(8,128)S(1)} %get-tuple-element.28.base_ref, ...), custom_call_target="tpu_custom_call" | custom-call | tf_op jit(solution)/shard_map/finish/pallas_call | solution.py:369
  64.4 17.1 %all_to_all.15.x_ref = bf16[32,20,128]{2,1,0:T(8,128)(2,1)S(1)} all-to-all(bf16[32,20,128]{2,1,0:T(8,128)(2,1)S(1)} %finish.1), channel_id=1, replica_groups=mesh['seg'=16,'grp'=32] {'grp'}, dimensions={0} | all-to-all | bytes 327680 | tf_op jit(solution)/shard_map/all_to_all | solution.py:403
  81.5 0.8 %unpack.1 = bf16[40,2048]{1,0:T(8,128)(2,1)} custom-call(bf16[32,20,128]{2,1,0:T(8,128)(2,1)S(1)} %all_to_all.15.x_ref), custom_call_target="tpu_custom_call" | custom-call | tf_op jit(solution)/shard_map/unpack/pallas_call | solution.py:393
Async XLA Ops:
  2.1 29.6 %all-to-all-start = ((bf16[32,64,128]{2,1,0:T(8,128)(2,1)}), bf16[32,64,128]{2,1,0:T(8,128)(2,1)S(1)}, u32[]{:S(2)}, u32[]{:S(2)}) async-start(bf16[32,64,128]{2,1,0:T(8,128)(2,1)} %pack.1), calls=%async_computation | async-start | bytes 1048576 | tf_op jit(solution)/shard_map/all_to_all | solution.py:403
  37.9 0.7 copy-start.2
  38.6 0.7 copy-start.4
  39.3 0.7 copy-start.6
  40.0 0.7 copy-start.8
  40.8 0.7 copy-start.10
  41.5 9.1 %copy-start.12 = (bf16[1280,128]{1,0:T(8,128)(2,1)}, bf16[1280,128]{1,0:T(8,128)(2,1)S(1)}, u32[]{:S(2)}) copy-start(bf16[1280,128]{1,0:T(8,128)(2,1)S(1)} %get-tuple-element.25.att_ref) | copy-start | bytes 983044
  41.5 20.3 %all-to-all-start.1 = ((bf16[16,64,128]{2,1,0:T(8,128)(2,1)}), bf16[16,64,128]{2,1,0:T(8,128)(2,1)S(1)}, u32[]{:S(2)}, u32[]{:S(2)}) async-start(bf16[16,64,128]{2,1,0:T(8,128)(2,1)} %get-tuple-element.18), calls=%async_computation.1 | async-start | bytes 524288 | tf_op jit(solution)/shard_map/all_to_all | solution.py:403
  50.6 1.0 %copy-start.3 = (bf16[1280,128]{1,0:T(8,128)(2,1)S(1)}, bf16[1280,128]{1,0:T(8,128)(2,1)}, u32[]{:S(2)}) copy-start(bf16[1280,128]{1,0:T(8,128)(2,1)} %copy-done.2) | copy-start | bytes 983044
  51.6 1.0 %copy-start.5 = (bf16[1280,128]{1,0:T(8,128)(2,1)S(1)}, bf16[1280,128]{1,0:T(8,128)(2,1)}, u32[]{:S(2)}) copy-start(bf16[1280,128]{1,0:T(8,128)(2,1)} %copy-done.4) | copy-start | bytes 983044
  52.6 1.0 %copy-start.7 = (bf16[1280,128]{1,0:T(8,128)(2,1)S(1)}, bf16[1280,128]{1,0:T(8,128)(2,1)}, u32[]{:S(2)}) copy-start(bf16[1280,128]{1,0:T(8,128)(2,1)} %copy-done.6) | copy-start | bytes 983044
  53.5 1.0 %copy-start.9 = (bf16[1280,128]{1,0:T(8,128)(2,1)S(1)}, bf16[1280,128]{1,0:T(8,128)(2,1)}, u32[]{:S(2)}) copy-start(bf16[1280,128]{1,0:T(8,128)(2,1)} %copy-done.8) | copy-start | bytes 983044
  54.5 1.0 %copy-start.11 = (bf16[1280,128]{1,0:T(8,128)(2,1)S(1)}, bf16[1280,128]{1,0:T(8,128)(2,1)}, u32[]{:S(2)}) copy-start(bf16[1280,128]{1,0:T(8,128)(2,1)} %copy-done.10) | copy-start | bytes 983044
  55.5 1.0 %copy-start.13 = (bf16[1280,128]{1,0:T(8,128)(2,1)S(1)}, bf16[1280,128]{1,0:T(8,128)(2,1)}, u32[]{:S(2)}) copy-start(bf16[1280,128]{1,0:T(8,128)(2,1)} %copy-done.12) | copy-start | bytes 983044
  56.5 5.4 %copy-start = (f32[1,64,64]{2,1,0:T(8,128)S(1)}, f32[1,64,64]{2,1,0:T(8,128)}, u32[]{:S(2)}) copy-start(f32[1,64,64]{2,1,0:T(8,128)} %sf_ref.1) | copy-start | bytes 49156
  56.5 5.4 %copy-start.1 = (f32[1,64,64]{2,1,0:T(8,128)S(1)}, f32[1,64,64]{2,1,0:T(8,128)}, u32[]{:S(2)}) copy-start(f32[1,64,64]{2,1,0:T(8,128)} %sb_ref.1) | copy-start | bytes 49156

commit v2 on v1

--- a/solution.py
+++ b/solution.py
@@ -12,6 +12,7 @@
 HDIM = 64
 LANES = 128
 QROWS = 256
+AROWS = 128
 VMEM_LIMIT = 24 * 1024 * 1024
 PACK_LIMIT = 62 * 1024 * 1024
 
@@ -115,9 +116,21 @@
     return jnp.where(row == lax.rem(col, HDIM), 1.0, 0.0).astype(f32)
 
 
+def norm_sums():
+    row = lax.broadcasted_iota(jnp.int32, (2 * LANES, 2 * LANES), 0)
+    col = lax.broadcasted_iota(jnp.int32, (2 * LANES, 2 * LANES), 1)
+    is_key_row = lax.rem(row, LANES) >= HDIM
+    return jnp.where(is_key_row == (col < LANES), 1.0, 0.0).astype(bf16)
+
+
+def inverse_norms(qk, sums):
+    hi, lo = split(qk * qk)
+    return lax.rsqrt(mm(jnp.concatenate([hi, lo], axis=1), sums) + 1e-06)
+
+
 def attend_body(
-    tv_ref, me_ref, recv_ref, msg_ref, q2_ref, k2_ref, ckh_ref, ckl_ref, dah_ref, dal_ref, att_ref, sq_ref, g_ref,
-    qk_scr, v_scr, r_scr, qs_scr, step_scr, kf_scr, kb_scr,
+    tv_ref, me_ref, recv_ref, msg_ref, qk_ref, ar_ref, g_ref,
+    qk_scr, v_scr, r_scr, inv_scr, rate_scr, k2_scr, qs_scr, kf_scr, kb_scr, da_scr, ckh_scr, ckl_scr,
 ):
     groups, rows, _ = recv_ref.shape
     toks = rows - 24
@@ -140,40 +153,36 @@
         v_scr[base + 24 : base + toks] = jnp.where(left_late, tail[0:late], tail_sw[0:late])
         r_scr[base : base + toks] = jnp.where(pick, tail[late : late + 1], 0.0)
 
-    row_id = lax.broadcasted_iota(jnp.int32, (2 * LANES, 2 * LANES), 0)
-    col_id = lax.broadcasted_iota(jnp.int32, (2 * LANES, 2 * LANES), 1)
-    is_key_row = lax.rem(row_id, LANES) >= HDIM
-    sums = jnp.where(is_key_row == (col_id < LANES), 1.0, 0.0).astype(bf16)
+    sums = norm_sums()
     ones = jnp.ones((LANES, LANES), bf16)
     left = lanes_left(QROWS)
-    cols = lax.broadcasted_iota(jnp.int32, (QROWS, TEXT), 1)
-
+
+    for b in range(blocks):
+        at = slice(QROWS * b, QROWS * (b + 1))
+        inv_scr[at] = inverse_norms(qk_scr[at], sums)[:, 0:LANES]
+        rate = mm(r_scr[at].astype(bf16), ones)
+        if QROWS * b < TEXT:
+            position = QROWS * b + lax.broadcasted_iota(jnp.int32, (QROWS, LANES), 0)
+            rate = jnp.where((position >= TEXT) | (position < valid), rate, 0.0)
+        rate_scr[at] = rate
     for b in range(blocks):
         at = slice(QROWS * b, QROWS * (b + 1))
         qk = qk_scr[at]
         kq = swap_halves(qk)
         k2 = jnp.where(left, kq, qk)
-        k2_ref[at] = k2.astype(bf16)
-        q2_ref[at] = jnp.where(left, qk, kq).astype(bf16)
+        k2_scr[at] = k2.astype(bf16)
+        qk_ref[at] = qk.astype(bf16)
         qs_scr[at] = jnp.where(left, qk * (1.0 / math.sqrt(HDIM)), 0.0).astype(bf16)
-        squares_hi, squares_lo = split(qk * qk)
-        inv = lax.rsqrt(mm(jnp.concatenate([squares_hi, squares_lo], axis=1), sums) + 1e-06)
-        inv_k = inv[:, 0:LANES]
-        sq_ref[at] = math.sqrt(HDIM) * inv[:, LANES : 2 * LANES]
-        rate = mm(r_scr[at].astype(bf16), ones)
-        if QROWS * b < TEXT:
-            position = QROWS * b + lax.broadcasted_iota(jnp.int32, (QROWS, LANES), 0)
-            rate = jnp.where((position >= TEXT) | (position < valid), rate, 0.0)
-        step = rate * inv_k
-        step_scr[at] = step
+        inv_k = inv_scr[at]
+        step = rate_scr[at] * inv_k
+        inv_scr[at] = step
         ck_hi, ck_lo = split(step * inv_k * k2)
-        ckh_ref[at] = ck_hi
-        ckl_ref[at] = ck_lo
-
+        ckh_scr[at] = ck_hi
+        ckl_scr[at] = ck_lo
     for n in range(chunks):
         at = slice(GROUP * n, GROUP * (n + 1))
-        k = k2_ref[at, 0:HDIM]
-        gram = mm_tn(jnp.concatenate([k, k], axis=0), jnp.concatenate([ckh_ref[at], ckl_ref[at]], axis=0))
+        k = k2_scr[at, 0:HDIM]
+        gram = mm_tn(jnp.concatenate([k, k], axis=0), jnp.concatenate([ckh_scr[at], ckl_scr[at]], axis=0))
         g_hi, g_lo = split(gram)
         g_ref[n, 0:HDIM] = g_hi
         g_ref[n, HDIM : 2 * HDIM] = g_lo
@@ -185,32 +194,36 @@
     def advance(t, n, keep_ref):
         at = slice(GROUP * n, GROUP * (n + 1))
         p = packed(t)
-        keep_ref[at] = packed(mm_nt(k2_ref[at], jnp.concatenate([p, p], axis=0)))
+        keep_ref[at] = packed(mm_nt(k2_scr[at], jnp.concatenate([p, p], axis=0)))
         return t - mm(twice(p), four(g_ref[n, 0:HDIM], g_ref[n, HDIM : 2 * HDIM]))
 
-    for b in range(blocks):
-        at = slice(QROWS * b, QROWS * (b + 1))
-        scores = mm_nt(qs_scr[at], k2_ref[...])
-        for n in range(chunks * b // blocks, chunks * (b + 1) // blocks):
+    parts = seglen // AROWS
+    cols = lax.broadcasted_iota(jnp.int32, (AROWS, TEXT), 1)
+    left_part = lanes_left(AROWS)
+
+    def scores_of(b):
+        scores = mm_nt(qs_scr[AROWS * b : AROWS * (b + 1)], k2_scr[...])
+        return jnp.concatenate([jnp.where(cols < valid, scores[:, 0:TEXT], -1e30), scores[:, TEXT:]], axis=1)
+
+    scores = scores_of(0)
+    for b in range(parts):
+        at = slice(AROWS * b, AROWS * (b + 1))
+        following = scores_of(b + 1) if b + 1 < parts else None
+        for n in range(chunks * b // parts, chunks * (b + 1) // parts):
             t_f = advance(t_f, n, kf_scr)
             t_b = advance(t_b, chunks - 1 - n, kb_scr)
-        head_part = jnp.where(cols < valid, scores[:, 0:TEXT], -1e30)
-        scores = jnp.concatenate([head_part, scores[:, TEXT:]], axis=1)
         peak = jnp.max(scores, axis=1, keepdims=True)
         raised = jnp.exp(scores - peak)
         row_total = jnp.sum(raised, axis=1, keepdims=True)
-        gathered = mm(raised.astype(bf16), v2)
-        att = (gathered / row_total).astype(bf16)
-        att_ref[at] = att
-        da_hi, da_lo = split(step_scr[at] * att.astype(f32))
-        dah_ref[at] = da_hi
-        dal_ref[at] = da_lo
+        att = (mm(raised.astype(bf16), v2) / row_total).astype(bf16).astype(f32)
+        ar_ref[at] = jnp.where(left_part, att, rate_scr[at]).astype(bf16)
+        da_scr[at] = packed(inv_scr[at] * att)
+        scores = following
 
     total = jnp.zeros((LANES, 2 * LANES), f32)
     for b in range(blocks):
         at = slice(QROWS * b, QROWS * (b + 1))
-        da = jnp.where(left, dah_ref[at].astype(f32), dal_ref[at].astype(f32)).astype(bf16)
-        total = total + mm_tn(da, jnp.concatenate([kf_scr[at], kb_scr[at]], axis=1))
+        total = total + mm_tn(da_scr[at], jnp.concatenate([kf_scr[at], kb_scr[at]], axis=1))
     total = total[0:HDIM] + total[HDIM : 2 * HDIM]
     from_f, from_b = total[:, 0:LANES], total[:, LANES : 2 * LANES]
     shift_b = from_f + swap_halves(from_f)
@@ -232,13 +245,12 @@
     return pl.pallas_call(
         attend_body,
         in_specs=[smem, smem, vmem],
-        out_specs=[vmem] * 10,
+        out_specs=[vmem] * 4,
         out_shape=[jax.ShapeDtypeStruct((segments, HDIM, LANES), link)]
-        + [jax.ShapeDtypeStruct(tall, bf16)] * 7
-        + [jax.ShapeDtypeStruct(tall, f32), jax.ShapeDtypeStruct((chunks, LANES, LANES), bf16)],
+        + [jax.ShapeDtypeStruct(tall, bf16)] * 2
+        + [jax.ShapeDtypeStruct((chunks, LANES, LANES), bf16)],
         scratch_shapes=[
-            pltpu.VMEM(tall, f32), pltpu.VMEM(tall, f32), pltpu.VMEM(tall, f32), pltpu.VMEM(tall, bf16),
-            pltpu.VMEM(tall, f32), pltpu.VMEM(tall, bf16), pltpu.VMEM(tall, bf16),
+            *[pltpu.VMEM(tall, f32)] * 5, *[pltpu.VMEM(tall, bf16)] * 7,
         ],
         compiler_params=pltpu.CompilerParams(vmem_limit_bytes=VMEM_LIMIT),
         name="attend",
@@ -246,13 +258,14 @@
 
 
 def operators_body(
-    q2_ref, k2_ref, ckh_ref, ckl_ref, dah_ref, dal_ref, att_ref, sq_ref, g_ref, base_ref, ehi_ref, elo_ref,
-    opf_scr, opb_scr, xf_scr, xb_scr,
+    qk_ref, ar_ref, g_ref, base_ref, ehi_ref, elo_ref,
+    opf_scr, opb_scr, xf_scr, xb_scr, shift_scr, yhi_scr, ylo_scr, k2_scr, q2_scr, inv_scr,
 ):
     chunks = g_ref.shape[0]
     row_id = lax.broadcasted_iota(jnp.int32, (GROUP, LANES), 0)
     col_id = lax.rem(lax.broadcasted_iota(jnp.int32, (GROUP, LANES), 1), GROUP)
     left = lanes_left(GROUP)
+    sums = norm_sums()
     eye = doubled_eye()
     x_f = jnp.concatenate([eye, jnp.zeros_like(eye)], axis=0)
     x_b = x_f
@@ -260,37 +273,60 @@
     def rows_of(n):
         return slice(GROUP * n, GROUP * (n + 1))
 
+    def halves(x):
+        x = x.astype(f32)
+        x_sw = swap_halves(x)
+        on_left = lanes_left(x.shape[0])
+        return jnp.where(on_left, x, x_sw), jnp.where(on_left, x_sw, x)
+
     def advance(x, n, keep_ref):
-        at = rows_of(n)
         hi, lo = split(x)
         keep_ref[n] = jnp.concatenate([hi, lo], axis=1)
         p = jnp.where(lanes_left(2 * HDIM), hi.astype(f32), lo.astype(f32)).astype(bf16)
-        k2 = k2_ref[at]
-        pushed = mm_tn(
-            jnp.concatenate([dah_ref[at, 0:HDIM], dal_ref[at, 0:HDIM]], axis=0), jnp.concatenate([k2, k2], axis=0)
-        )
         x = x - mm(twice(p), four(g_ref[n, 0:HDIM], g_ref[n, HDIM : 2 * HDIM]))
-        return jnp.concatenate([x[0:HDIM], x[HDIM : 2 * HDIM] + pushed], axis=0)
+        return jnp.concatenate([x[0:HDIM], x[HDIM : 2 * HDIM] + shift_scr[n]], axis=0)
+
+    blocks = chunks * GROUP // QROWS
+    for b in range(blocks):
+        at = slice(QROWS * b, QROWS * (b + 1))
+        inv_scr[at] = inverse_norms(qk_ref[at].astype(f32), sums)
+    for b in range(blocks):
+        at = slice(QROWS * b, QROWS * (b + 1))
+        inv_k = inv_scr[at, 0:LANES]
+        q2, k2 = halves(qk_ref[at])
+        att, rate = halves(ar_ref[at])
+        step = rate * inv_k
+        ck_hi, ck_lo = split(step * inv_k * k2)
+        da_hi, da_lo = split(step * att)
+        yhi_scr[at] = jnp.concatenate([ck_hi, da_hi], axis=1)
+        ylo_scr[at] = jnp.concatenate([ck_lo, da_lo], axis=1)
+        base_ref[at] = att
+        q2_scr[at] = q2.astype(bf16)
+        k2_scr[at] = k2.astype(bf16)
+    for n in range(chunks):
+        at = rows_of(n)
+        k2 = k2_scr[at]
+        da = jnp.concatenate([yhi_scr[at, LANES : LANES + HDIM], ylo_scr[at, LANES : LANES + HDIM]], axis=0)
+        shift_scr[n] = mm_tn(da, jnp.concatenate([k2, k2], axis=0))
 
     for n in range(chunks):
         x_f = advance(x_f, n, xf_scr)
         x_b = advance(x_b, chunks - 1 - n, xb_scr)
         at = rows_of(n)
-        k2, q2 = k2_ref[at], q2_ref[at]
+        q2, k2 = q2_scr[at], k2_scr[at]
         scores = mm_nt(q2[:, 0:HDIM], jnp.concatenate([k2, k2], axis=0)[:, 0:HDIM])
         both = packed(
             jnp.concatenate(
                 [jnp.where(col_id <= row_id, scores, 0.0), jnp.where(col_id >= row_id, scores, 0.0)], axis=0
             )
         )
-        y_hi = jnp.concatenate([ckh_ref[at], dah_ref[at]], axis=1)
-        y_lo = jnp.concatenate([ckl_ref[at], dal_ref[at]], axis=1)
+        y_hi, y_lo = yhi_scr[at], ylo_scr[at]
         pushed = mm(twice(both), four(y_hi, y_lo))
-        scale = sq_ref[at]
+        scale = math.sqrt(HDIM) * inv_scr[at, LANES : 2 * LANES]
         q = q2.astype(f32)
         opf_scr[at] = packed(scale * (q - pushed[0:GROUP, 0:LANES]))
         opb_scr[at] = packed(scale * (q - pushed[GROUP : 2 * GROUP, 0:LANES]))
-        base_ref[at] = att_ref[at].astype(f32) + scale * (
+        base_ref[at] = base_ref[at] + scale * (
             pushed[0:GROUP, LANES : 2 * LANES] + pushed[GROUP : 2 * GROUP, LANES : 2 * LANES]
         )
 
@@ -321,6 +357,9 @@
         ],
         scratch_shapes=[
             pltpu.VMEM(tall, bf16), pltpu.VMEM(tall, bf16), pltpu.VMEM(state, bf16), pltpu.VMEM(state, bf16),
+            pltpu.VMEM((chunks, HDIM, LANES), f32),
+            pltpu.VMEM((tall[0], 2 * LANES), bf16), pltpu.VMEM((tall[0], 2 * LANES), bf16),
+            pltpu.VMEM(tall, bf16), pltpu.VMEM(tall, bf16), pltpu.VMEM((tall[0], 2 * LANES), f32),
         ],
         compiler_params=pltpu.CompilerParams(vmem_limit_bytes=VMEM_LIMIT),
         cost_estimate=pl.CostEstimate(flops=2_000_000_000, bytes_accessed=8_000_000, transcendentals=0),

time: 82.9 us -> 78.7 us (0.949)
  local copies, waits for them, and re-layouts: 9.48 us -> 0.01 us
  waiting for transfers between devices: 17.1 us -> 21.7 us
    unnamed x28 -> x4, local copies, waits for them, and re-layouts: 9.48 us -> 0.01 us
    all_to_all x2, waiting for transfers between devices: 17.1 us -> 21.7 us  [exchange(): return lax.all_to_all(x, axis, split_axis=0, concat_axis=0, tiled=True)]
    pallas_call x1, Pallas kernels: 4.35 us -> 5.54 us  [operators(): pl.pallas_call(operators_body, out_shape=[jax.ShapeDtypeStruct(tall, f32)...]
  transfers between devices with their start and end apart: 2 -> 2, of which waited for: 2 -> 2; matrix products, arithmetic and copies ran while one was open for 0% -> 0% of each run, Pallas kernels for 5% -> 7%
where the time goes in v2:
time: 78.7 us; the launch traced here: 78.3 us
  starting transfers between devices  22 us (28%)
  waiting for transfers between devices  21.7 us (28%)
  blocking collectives  17.1 us (22%)
  Pallas kernels  16.7 us (21%)
    all_to_all x2, starting transfers between devices, exchange(): return lax.all_to_all(x, axis, split_axis=0, concat_axis=0, tiled=True)  22 us
    all_to_all x2, waiting for transfers between devices, exchange(): return lax.all_to_all(x, axis, split_axis=0, concat_axis=0, tiled=True)  21.7 us
    all_to_all x1, blocking collectives, exchange(): return lax.all_to_all(x, axis, split_axis=0, concat_axis=0, tiled=True)  17.1 us
    pallas_call x1, Pallas kernels, attend(): pl.pallas_call(attend_body, in_specs=[smem, smem, vmem], out_specs=[vmem]...  5.71 us
    pallas_call x1, Pallas kernels, operators(): pl.pallas_call(operators_body, out_shape=[jax.ShapeDtypeStruct(tall, f32)...  5.54 us
    pallas_call x1, Pallas kernels, finish(): pl.pallas_call(finish_body, in_specs=[smem] + [vmem] * 6, out_specs=vmem,...  2.51 us
    pallas_call x1, Pallas kernels, pack(): pl.pallas_call(pack_body, in_specs=[pl.BlockSpec(memory_space=pl.ANY)] *...  2.11 us
  transfers between devices with their start and end apart: 2, of which 2 were waited for; matrix products, arithmetic and copies ran while one was open for 0% of the time, Pallas kernels for 7%

profile of v2, /device:TPU:1, one launch (start us, length us, event | category | flops | bytes accessed | tf_op | source)
XLA Modules:
  0.0 78.3 jit_solution(153817840659683922)
XLA Ops:
  0.0 2.1 %pack.1 = bf16[32,64,128]{2,1,0:T(8,128)(2,1)} custom-call(bf16[40,2048]{1,0:T(8,128)(2,1)} %q_hbm.1, bf16[40,2048]{1,0:T(8,128)(2,1)} %k_hbm.1, bf16[40,2048]{1,0:T(8,128)(2,1)} %v_hbm.1, bf16[32,40]{1,0:T(8,128)(2,1)} %bitcast.2), custom_call_target="tpu_custom_call" | custom-call | tf_op jit(solution)/shard_map/pack/pallas_call | solution.py:83
  2.1 12.9 %all-to-all-start = ((bf16[32,64,128]{2,1,0:T(8,128)(2,1)}), bf16[32,64,128]{2,1,0:T(8,128)(2,1)S(1)}, u32[]{:S(2)}, u32[]{:S(2)}) async-start(bf16[32,64,128]{2,1,0:T(8,128)(2,1)} %pack.1), calls=%async_computation | async-start | bytes 1048576 | tf_op jit(solution)/shard_map/all_to_all | solution.py:442
  15.7 16.1 %all-to-all-done.recv_ref = bf16[32,64,128]{2,1,0:T(8,128)(2,1)S(1)} async-done(((bf16[32,64,128]{2,1,0:T(8,128)(2,1)}), bf16[32,64,128]{2,1,0:T(8,128)(2,1)S(1)}, u32[]{:S(2)}, u32[]{:S(2)}) %all-to-all-start) | async-done | bytes 524320 | tf_op jit(solution)/shard_map/all_to_all | solution.py:442
  31.8 5.7 %attend.1 = (bf16[16,64,128]{2,1,0:T(8,128)(2,1)}, bf16[1280,128]{1,0:T(8,128)(2,1)S(1)}, bf16[1280,128]{1,0:T(8,128)(2,1)S(1)}, bf16[20,128,128]{2,1,0:T(8,128)(2,1)S(1)}) custom-call(s32[1]{0:T(128)S(6)} %copy.8.tv_ref, s32[1]{0:T(128)} %bitcast.me_ref, bf16[32,64,128]{2,1,0:T(8,128)(2,1)S(1)} %all-to-all-done.recv_ref), custom_call_target="tpu_custom_call" | custom-call | tf_op jit(solution)/shard_map/attend/pallas_call | solution.py:245
  37.5 9.1 %all-to-all-start.1 = ((bf16[16,64,128]{2,1,0:T(8,128)(2,1)}), bf16[16,64,128]{2,1,0:T(8,128)(2,1)S(1)}, u32[]{:S(2)}, u32[]{:S(2)}) async-start(bf16[16,64,128]{2,1,0:T(8,128)(2,1)} %get-tuple-element.12), calls=%async_computation.1 | async-start | bytes 524288 | tf_op jit(solution)/shard_map/all_to_all | solution.py:442
  46.6 0.0 copy-start
  46.6 0.0 copy-start.1
  46.6 5.5 %operators.1 = (f32[1280,128]{1,0:T(8,128)S(1)}, bf16[1280,128]{1,0:T(8,128)(2,1)S(1)}, bf16[1280,128]{1,0:T(8,128)(2,1)S(1)}) custom-call(bf16[1280,128]{1,0:T(8,128)(2,1)S(1)} %get-tuple-element.13.qk_ref, bf16[1280,128]{1,0:T(8,128)(2,1)S(1)} %get-tuple-element.14.ar_ref, bf16[20,128,128]{2,1,0:T(8,128)(2,1)S(1)} %get-tuple-element.15.g_ref), custom_call_target="tpu_custom_call" | custom-call | flops 2000000000 | bytes 8000000 | tf_op jit(solution)/shard_map/operators/pallas_call | solution.py:351
  52.1 5.7 %all-to-all-done.1.msg_ref = bf16[16,64,128]{2,1,0:T(8,128)(2,1)S(1)} async-done(((bf16[16,64,128]{2,1,0:T(8,128)(2,1)}), bf16[16,64,128]{2,1,0:T(8,128)(2,1)S(1)}, u32[]{:S(2)}, u32[]{:S(2)}) %all-to-all-start.1) | async-done | bytes 262176 | tf_op jit(solution)/shard_map/all_to_all | solution.py:442
  57.8 0.0 copy-done
  57.8 0.0 copy-done.1
  57.8 2.5 %finish.1 = bf16[32,20,128]{2,1,0:T(8,128)(2,1)S(1)} custom-call(s32[1]{0:T(128)} %bitcast.me_ref, bf16[16,64,128]{2,1,0:T(8,128)(2,1)S(1)} %all-to-all-done.1.msg_ref, f32[1,64,64]{2,1,0:T(8,128)S(1)} %copy-done, f32[1,64,64]{2,1,0:T(8,128)S(1)} %copy-done.1, f32[1280,128]{1,0:T(8,128)S(1)} %get-tuple-element.16.base_ref, ...), custom_call_target="tpu_custom_call" | custom-call | tf_op jit(solution)/shard_map/finish/pallas_call | solution.py:408
  60.3 17.1 %all_to_all.15.x_ref = bf16[32,20,128]{2,1,0:T(8,128)(2,1)S(1)} all-to-all(bf16[32,20,128]{2,1,0:T(8,128)(2,1)S(1)} %finish.1), channel_id=1, replica_groups=mesh['seg'=16,'grp'=32] {'grp'}, dimensions={0} | all-to-all | bytes 327680 | tf_op jit(solution)/shard_map/all_to_all | solution.py:442
  77.4 0.8 %unpack.1 = bf16[40,2048]{1,0:T(8,128)(2,1)} custom-call(bf16[32,20,128]{2,1,0:T(8,128)(2,1)S(1)} %all_to_all.15.x_ref), custom_call_target="tpu_custom_call" | custom-call | tf_op jit(solution)/shard_map/unpack/pallas_call | solution.py:432
Async XLA Ops:
  2.1 29.6 %all-to-all-start = ((bf16[32,64,128]{2,1,0:T(8,128)(2,1)}), bf16[32,64,128]{2,1,0:T(8,128)(2,1)S(1)}, u32[]{:S(2)}, u32[]{:S(2)}) async-start(bf16[32,64,128]{2,1,0:T(8,128)(2,1)} %pack.1), calls=%async_computation | async-start | bytes 1048576 | tf_op jit(solution)/shard_map/all_to_all | solution.py:442
  37.5 20.3 %all-to-all-start.1 = ((bf16[16,64,128]{2,1,0:T(8,128)(2,1)}), bf16[16,64,128]{2,1,0:T(8,128)(2,1)S(1)}, u32[]{:S(2)}, u32[]{:S(2)}) async-start(bf16[16,64,128]{2,1,0:T(8,128)(2,1)} %get-tuple-element.12), calls=%async_computation.1 | async-start | bytes 524288 | tf_op jit(solution)/shard_map/all_to_all | solution.py:442
  46.6 11.2 %copy-start = (f32[1,64,64]{2,1,0:T(8,128)S(1)}, f32[1,64,64]{2,1,0:T(8,128)}, u32[]{:S(2)}) copy-start(f32[1,64,64]{2,1,0:T(8,128)} %sf_ref.1) | copy-start | bytes 49156
  46.6 11.2 %copy-start.1 = (f32[1,64,64]{2,1,0:T(8,128)S(1)}, f32[1,64,64]{2,1,0:T(8,128)}, u32[]{:S(2)}) copy-start(f32[1,64,64]{2,1,0:T(8,128)} %sb_ref.1) | copy-start | bytes 49156

commit v3 on v2

--- a/solution.py
+++ b/solution.py
@@ -13,6 +13,7 @@
 LANES = 128
 QROWS = 256
 AROWS = 128
+PACK_PARTS = 2
 VMEM_LIMIT = 24 * 1024 * 1024
 PACK_LIMIT = 62 * 1024 * 1024
 
@@ -45,36 +46,54 @@
     return pltpu.roll(x, HDIM, 1)
 
 
-def pack_body(q_hbm, k_hbm, v_hbm, r_hbm, o_ref, q_ref, k_ref, v_ref, r_ref, rate_scr, sems):
-    copies = [
-        pltpu.make_async_copy(source, target, sems.at[i])
-        for i, (source, target) in enumerate(((r_hbm, r_ref), (q_hbm, q_ref), (k_hbm, k_ref), (v_hbm, v_ref)))
-    ]
-    for copy in copies:
-        copy.start()
+def pack_body(q_hbm, k_hbm, v_hbm, r_hbm, o_hbm, q_ref, k_ref, v_ref, r_ref, o_ref, rate_scr, in_sems, out_sems):
     rows, width = q_ref.shape
     heads = width // HDIM
     late = rows - 24
+    parts = in_sems.shape[0]
+    wide = width // parts
+    each = heads // parts
+    rate_copy = pltpu.make_async_copy(r_hbm, r_ref, in_sems.at[0, 3])
+    rate_copy.start()
+    reads, writes = [], []
+    for part in range(parts):
+        cols = pl.ds(wide * part, wide)
+        reads.append(
+            [
+                pltpu.make_async_copy(source.at[:, cols], target.at[:, cols], in_sems.at[part, i])
+                for i, (source, target) in enumerate(((q_hbm, q_ref), (k_hbm, k_ref), (v_hbm, v_ref)))
+            ]
+        )
+        for read in reads[part]:
+            read.start()
     left = lanes_left(rows)
     left24 = lanes_left(24)
     rate_scr[...] = jnp.zeros_like(rate_scr)
-    for copy in copies:
-        copy.wait()
+    rate_copy.wait()
     rate_scr[:, 0:rows] = r_ref[...].astype(f32)
-    for p in range(heads // 2):
-        cols = slice(LANES * p, LANES * (p + 1))
-        q = q_ref[:, cols].astype(f32)
-        k = k_ref[:, cols].astype(f32)
-        v = v_ref[:, cols].astype(f32)
-        q_sw, k_sw, v_sw = swap_halves(q), swap_halves(k), swap_halves(v)
-        for odd in (0, 1):
-            head = 2 * p + odd
-            qk = jnp.where(left, q_sw, k) if odd else jnp.where(left, q, k_sw)
-            v_right, v_left = (v, v_sw) if odd else (v_sw, v)
-            rate = jnp.broadcast_to(rate_scr[head : head + 1, :], (24 - late, LANES))
-            low = jnp.concatenate([v_left[24:rows], rate], axis=0)
-            vr = jnp.where(left24, low, v_right[0:24])
-            o_ref[head] = jnp.concatenate([qk, vr], axis=0).astype(bf16)
+    for part in range(parts):
+        for read in reads[part]:
+            read.wait()
+        for p in range(each // 2 * part, each // 2 * (part + 1)):
+            cols = slice(LANES * p, LANES * (p + 1))
+            q = q_ref[:, cols].astype(f32)
+            k = k_ref[:, cols].astype(f32)
+            v = v_ref[:, cols].astype(f32)
+            q_sw, k_sw, v_sw = swap_halves(q), swap_halves(k), swap_halves(v)
+            for odd in (0, 1):
+                head = 2 * p + odd
+                qk = jnp.where(left, q_sw, k) if odd else jnp.where(left, q, k_sw)
+                v_right, v_left = (v, v_sw) if odd else (v_sw, v)
+                rate = jnp.broadcast_to(rate_scr[head : head + 1, :], (24 - late, LANES))
+                low = jnp.concatenate([v_left[24:rows], rate], axis=0)
+                vr = jnp.where(left24, low, v_right[0:24])
+                o_ref[head] = jnp.concatenate([qk, vr], axis=0).astype(bf16)
+        own = pl.ds(each * part, each)
+        write = pltpu.make_async_copy(o_ref.at[own], o_hbm.at[own], out_sems.at[part])
+        write.start()
+        writes.append(write)
+    for write in writes:
+        write.wait()
 
 
 def pack(queries, keys, values, rates_t):
@@ -83,14 +102,17 @@
     return pl.pallas_call(
         pack_body,
         in_specs=[pl.BlockSpec(memory_space=pl.ANY)] * 4,
+        out_specs=pl.BlockSpec(memory_space=pl.ANY),
         out_shape=jax.ShapeDtypeStruct((heads, rows + 24, LANES), bf16),
         scratch_shapes=[
             pltpu.VMEM((rows, width), bf16),
             pltpu.VMEM((rows, width), bf16),
             pltpu.VMEM((rows, width), bf16),
             pltpu.VMEM((heads, rows), bf16),
+            pltpu.VMEM((heads, rows + 24, LANES), bf16),
             pltpu.VMEM((heads, LANES), f32),
-            pltpu.SemaphoreType.DMA((4,)),
+            pltpu.SemaphoreType.DMA((PACK_PARTS, 4)),
+            pltpu.SemaphoreType.DMA((PACK_PARTS,)),
         ],
         compiler_params=pltpu.CompilerParams(vmem_limit_bytes=PACK_LIMIT),
         name="pack",
@@ -130,7 +152,7 @@
 
 def attend_body(
     tv_ref, me_ref, recv_ref, msg_ref, qk_ref, ar_ref, g_ref,
-    qk_scr, v_scr, r_scr, inv_scr, rate_scr, k2_scr, qs_scr, kf_scr, kb_scr, da_scr, ckh_scr, ckl_scr,
+    qk_scr, v_scr, r_scr, inv_scr, rate_scr, k2_scr, qs_scr, tf_scr, tb_scr, da_scr, ckh_scr, ckl_scr, h_scr,
 ):
     groups, rows, _ = recv_ref.shape
     toks = rows - 24
@@ -191,11 +213,32 @@
     eye = doubled_eye()
     t_f, t_b = eye, eye
 
-    def advance(t, n, keep_ref):
-        at = slice(GROUP * n, GROUP * (n + 1))
+    def gram_right(n):
+        return four(g_ref[n, 0:HDIM], g_ref[n, HDIM : 2 * HDIM])
+
+    for m in range(chunks // 2):
+        g0, g1 = (g_ref[2 * m + i, 0:HDIM].astype(f32) + g_ref[2 * m + i, HDIM : 2 * HDIM].astype(f32) for i in (0, 1))
+        pair = g0 + g1 - mm(twice(packed(g0)), gram_right(2 * m + 1))
+        hi, lo = split(pair)
+        h_scr[m, 0:HDIM] = hi
+        h_scr[m, HDIM : 2 * HDIM] = lo
+
+    def advance_f(t, m):
         p = packed(t)
-        keep_ref[at] = packed(mm_nt(k2_scr[at], jnp.concatenate([p, p], axis=0)))
-        return t - mm(twice(p), four(g_ref[n, 0:HDIM], g_ref[n, HDIM : 2 * HDIM]))
+        keep(tf_scr, 2 * m, p)
+        keep(tf_scr, 2 * m + 1, packed(t - mm(twice(p), gram_right(2 * m))))
+        return t - mm(twice(p), four(h_scr[m, 0:HDIM], h_scr[m, HDIM : 2 * HDIM]))
+
+    def advance_b(t, m):
+        p = packed(t)
+        keep(tb_scr, 2 * m + 1, p)
+        keep(tb_scr, 2 * m, packed(t - mm(twice(p), gram_right(2 * m + 1))))
+        hi, lo = h_scr[m, 0:HDIM], h_scr[m, HDIM : 2 * HDIM]
+        row = jnp.concatenate([hi, lo], axis=1)
+        return t - mm_nt(twice(p), jnp.concatenate([row, row], axis=0))
+
+    def keep(ref, n, p):
+        ref[GROUP * n : GROUP * (n + 1)] = p
 
     parts = seglen // AROWS
     cols = lax.broadcasted_iota(jnp.int32, (AROWS, TEXT), 1)
@@ -209,9 +252,9 @@
     for b in range(parts):
         at = slice(AROWS * b, AROWS * (b + 1))
         following = scores_of(b + 1) if b + 1 < parts else None
-        for n in range(chunks * b // parts, chunks * (b + 1) // parts):
-            t_f = advance(t_f, n, kf_scr)
-            t_b = advance(t_b, chunks - 1 - n, kb_scr)
+        for m in range(chunks // 2 * b // parts, chunks // 2 * (b + 1) // parts):
+            t_f = advance_f(t_f, m)
+            t_b = advance_b(t_b, chunks // 2 - 1 - m)
         peak = jnp.max(scores, axis=1, keepdims=True)
         raised = jnp.exp(scores - peak)
         row_total = jnp.sum(raised, axis=1, keepdims=True)
@@ -222,12 +265,16 @@
 
     total = jnp.zeros((LANES, 2 * LANES), f32)
     for b in range(blocks):
+        reach = []
+        for n in range(QROWS // GROUP * b, QROWS // GROUP * (b + 1)):
+            at = slice(GROUP * n, GROUP * (n + 1))
+            hi, lo = split(mm_nt(k2_scr[at], jnp.concatenate([tf_scr[at], tb_scr[at]], axis=0)))
+            reach.append(jnp.concatenate([hi, lo], axis=1))
         at = slice(QROWS * b, QROWS * (b + 1))
-        total = total + mm_tn(da_scr[at], jnp.concatenate([kf_scr[at], kb_scr[at]], axis=1))
+        total = total + mm_tn(da_scr[at], jnp.concatenate(reach, axis=0))
     total = total[0:HDIM] + total[HDIM : 2 * HDIM]
-    from_f, from_b = total[:, 0:LANES], total[:, LANES : 2 * LANES]
-    shift_b = from_f + swap_halves(from_f)
-    shift_f = from_b + swap_halves(from_b)
+    shift_f = total[:, 0:LANES] + total[:, LANES : 2 * LANES]
+    shift_b = swap_halves(shift_f)
     left64 = lanes_left(HDIM)
     later = jnp.where(left64, t_f - eye, shift_f)
     earlier = jnp.where(left64, t_b - eye, shift_b)
@@ -250,7 +297,7 @@
         + [jax.ShapeDtypeStruct(tall, bf16)] * 2
         + [jax.ShapeDtypeStruct((chunks, LANES, LANES), bf16)],
         scratch_shapes=[
-            *[pltpu.VMEM(tall, f32)] * 5, *[pltpu.VMEM(tall, bf16)] * 7,
+            *[pltpu.VMEM(tall, f32)] * 5, *[pltpu.VMEM(tall, bf16)] * 7, pltpu.VMEM((chunks // 2, LANES, LANES), bf16),
         ],
         compiler_params=pltpu.CompilerParams(vmem_limit_bytes=VMEM_LIMIT),
         name="attend",
@@ -313,8 +360,8 @@
         x_f = advance(x_f, n, xf_scr)
         x_b = advance(x_b, chunks - 1 - n, xb_scr)
         at = rows_of(n)
-        q2, k2 = q2_scr[at], k2_scr[at]
-        scores = mm_nt(q2[:, 0:HDIM], jnp.concatenate([k2, k2], axis=0)[:, 0:HDIM])
+        q2, k2 = q2_scr[at].astype(f32), k2_scr[at]
+        scores = mm_nt(jnp.where(left, q2, 0.0).astype(bf16), jnp.concatenate([k2, k2], axis=0))
         both = packed(
             jnp.concatenate(
                 [jnp.where(col_id <= row_id, scores, 0.0), jnp.where(col_id >= row_id, scores, 0.0)], axis=0
@@ -323,9 +370,8 @@
         y_hi, y_lo = yhi_scr[at], ylo_scr[at]
         pushed = mm(twice(both), four(y_hi, y_lo))
         scale = math.sqrt(HDIM) * inv_scr[at, LANES : 2 * LANES]
-        q = q2.astype(f32)
-        opf_scr[at] = packed(scale * (q - pushed[0:GROUP, 0:LANES]))
-        opb_scr[at] = packed(scale * (q - pushed[GROUP : 2 * GROUP, 0:LANES]))
+        opf_scr[at] = packed(scale * (q2 - pushed[0:GROUP, 0:LANES]))
+        opb_scr[at] = packed(scale * (q2 - pushed[GROUP : 2 * GROUP, 0:LANES]))
         base_ref[at] = base_ref[at] + scale * (
             pushed[0:GROUP, LANES : 2 * LANES] + pushed[GROUP : 2 * GROUP, LANES : 2 * LANES]
         )
@@ -376,18 +422,32 @@
     def doubled_transpose(state):
         return jnp.concatenate([state, state], axis=0).T
 
-    def follow(i, live, state):
-        m = jnp.where(live, msg_ref[i].astype(f32), 0.0)
+    def times(x, decay):
+        return mm(twice(packed(x)), four(*split(decay)))
+
+    def leaf(i):
+        m = msg_ref[i].astype(f32)
         m_sw = swap_halves(m)
-        decay = jnp.where(left64, m, m_sw)
-        shift = jnp.where(left64, m_sw, m)
-        hi, lo = split(decay)
-        return state + mm(twice(packed(state)), four(hi, lo)) + shift
+        return jnp.concatenate([jnp.where(left64, m, m_sw), jnp.where(left64, m_sw, m)], axis=0)
+
+    def then(first, second):
+        return first + second + times(first, second[0:HDIM])
+
+    def sibling(level):
+        size = 2**level
+        block = lax.div(me, size)
+        before = lax.rem(block, 2) == 1
+        start = jnp.where(before, block - 1, block + 1) * size
+        nodes = [leaf(start + jnp.where(before, i, size - 1 - i)) for i in range(size)]
+        while len(nodes) > 1:
+            nodes = [then(nodes[i], nodes[i + 1]) for i in range(0, len(nodes), 2)]
+        return before, nodes[0]
 
     w_f, w_b = doubled_transpose(sf_ref[0]), doubled_transpose(sb_ref[0])
-    for i in range(segments - 1):
-        w_f = follow(i, i < me, w_f)
-        w_b = follow(segments - 1 - i, segments - 1 - i > me, w_b)
+    for before, node in [sibling(level) for level in reversed(range(segments.bit_length() - 1))]:
+        state = jnp.where(before, w_f, w_b)
+        state = state + times(state, node[0:HDIM]) + node[HDIM : 2 * HDIM]
+        w_f, w_b = jnp.where(before, state, w_f), jnp.where(before, w_b, state)
     w_hi, w_lo = split(jnp.where(left64, w_f, w_b))
     w_row = jnp.concatenate([w_hi, w_hi, w_lo], axis=1)
     e_hi = ehi_ref[...]

time: 78.7 us -> 77.3 us (0.982)
  Pallas kernels: 16.7 us -> 15.3 us
    pallas_call x1, Pallas kernels: 2.51 us -> 1.62 us  [finish(): pl.pallas_call(finish_body, in_specs=[smem] + [vmem] * 6, out_specs=vmem,...]
where the time goes in v3:
time: 77.3 us; the launch traced here: 76.8 us
  starting transfers between devices  22 us (28%)
  waiting for transfers between devices  21.7 us (28%)
  blocking collectives  17.1 us (22%)
  Pallas kernels  15.3 us (20%)
    all_to_all x2, starting transfers between devices, exchange(): return lax.all_to_all(x, axis, split_axis=0, concat_axis=0, tiled=True)  22 us
    all_to_all x2, waiting for transfers between devices, exchange(): return lax.all_to_all(x, axis, split_axis=0, concat_axis=0, tiled=True)  21.7 us
    all_to_all x1, blocking collectives, exchange(): return lax.all_to_all(x, axis, split_axis=0, concat_axis=0, tiled=True)  17.1 us
    pallas_call x1, Pallas kernels, operators(): pl.pallas_call(operators_body, out_shape=[jax.ShapeDtypeStruct(tall, f32)...  5.58 us
    pallas_call x1, Pallas kernels, attend(): pl.pallas_call(attend_body, in_specs=[smem, smem, vmem], out_specs=[vmem]...  5.24 us
    pallas_call x1, Pallas kernels, pack(): pl.pallas_call(pack_body, in_specs=[pl.BlockSpec(memory_space=pl.ANY)] *...  2.04 us
    pallas_call x1, Pallas kernels, finish(): pl.pallas_call(finish_body, in_specs=[smem] + [vmem] * 6, out_specs=vmem,...  1.62 us
  transfers between devices with their start and end apart: 2, of which 2 were waited for; matrix products, arithmetic and copies ran while one was open for 0% of the time, Pallas kernels for 7%

profile of v3, /device:TPU:1, one launch (start us, length us, event | category | flops | bytes accessed | tf_op | source)
XLA Modules:
  0.0 76.8 jit_solution(7538113341887101064)
XLA Ops:
  0.0 2.0 %pack.1 = bf16[32,64,128]{2,1,0:T(8,128)(2,1)} custom-call(bf16[40,2048]{1,0:T(8,128)(2,1)} %q_hbm.1, bf16[40,2048]{1,0:T(8,128)(2,1)} %k_hbm.1, bf16[40,2048]{1,0:T(8,128)(2,1)} %v_hbm.1, bf16[32,40]{1,0:T(8,128)(2,1)} %bitcast.2), custom_call_target="tpu_custom_call" | custom-call | tf_op jit(solution)/shard_map/pack/pallas_call | solution.py:102
  2.0 12.9 %all-to-all-start = ((bf16[32,64,128]{2,1,0:T(8,128)(2,1)}), bf16[32,64,128]{2,1,0:T(8,128)(2,1)S(1)}, u32[]{:S(2)}, u32[]{:S(2)}) async-start(bf16[32,64,128]{2,1,0:T(8,128)(2,1)} %pack.1), calls=%async_computation | async-start | bytes 1048576 | tf_op jit(solution)/shard_map/all_to_all | solution.py:502
  15.6 16.1 %all-to-all-done.recv_ref = bf16[32,64,128]{2,1,0:T(8,128)(2,1)S(1)} async-done(((bf16[32,64,128]{2,1,0:T(8,128)(2,1)}), bf16[32,64,128]{2,1,0:T(8,128)(2,1)S(1)}, u32[]{:S(2)}, u32[]{:S(2)}) %all-to-all-start) | async-done | bytes 524320 | tf_op jit(solution)/shard_map/all_to_all | solution.py:502
  31.7 5.2 %attend.1 = (bf16[16,64,128]{2,1,0:T(8,128)(2,1)}, bf16[1280,128]{1,0:T(8,128)(2,1)S(1)}, bf16[1280,128]{1,0:T(8,128)(2,1)S(1)}, bf16[20,128,128]{2,1,0:T(8,128)(2,1)S(1)}) custom-call(s32[1]{0:T(128)S(6)} %copy.8.tv_ref, s32[1]{0:T(128)} %bitcast.me_ref, bf16[32,64,128]{2,1,0:T(8,128)(2,1)S(1)} %all-to-all-done.recv_ref), custom_call_target="tpu_custom_call" | custom-call | tf_op jit(solution)/shard_map/attend/pallas_call | solution.py:292
  36.9 9.1 %all-to-all-start.1 = ((bf16[16,64,128]{2,1,0:T(8,128)(2,1)}), bf16[16,64,128]{2,1,0:T(8,128)(2,1)S(1)}, u32[]{:S(2)}, u32[]{:S(2)}) async-start(bf16[16,64,128]{2,1,0:T(8,128)(2,1)} %get-tuple-element.12), calls=%async_computation.1 | async-start | bytes 524288 | tf_op jit(solution)/shard_map/all_to_all | solution.py:502
  46.0 0.0 copy-start
  46.0 0.0 copy-start.1
  46.0 5.6 %operators.1 = (f32[1280,128]{1,0:T(8,128)S(1)}, bf16[1280,128]{1,0:T(8,128)(2,1)S(1)}, bf16[1280,128]{1,0:T(8,128)(2,1)S(1)}) custom-call(bf16[1280,128]{1,0:T(8,128)(2,1)S(1)} %get-tuple-element.13.qk_ref, bf16[1280,128]{1,0:T(8,128)(2,1)S(1)} %get-tuple-element.14.ar_ref, bf16[20,128,128]{2,1,0:T(8,128)(2,1)S(1)} %get-tuple-element.15.g_ref), custom_call_target="tpu_custom_call" | custom-call | flops 2000000000 | bytes 8000000 | tf_op jit(solution)/shard_map/operators/pallas_call | solution.py:397
  51.6 5.6 %all-to-all-done.1.msg_ref = bf16[16,64,128]{2,1,0:T(8,128)(2,1)S(1)} async-done(((bf16[16,64,128]{2,1,0:T(8,128)(2,1)}), bf16[16,64,128]{2,1,0:T(8,128)(2,1)S(1)}, u32[]{:S(2)}, u32[]{:S(2)}) %all-to-all-start.1) | async-done | bytes 262176 | tf_op jit(solution)/shard_map/all_to_all | solution.py:502
  57.3 0.0 copy-done
  57.3 0.0 copy-done.1
  57.3 1.6 %finish.1 = bf16[32,20,128]{2,1,0:T(8,128)(2,1)S(1)} custom-call(s32[1]{0:T(128)} %bitcast.me_ref, bf16[16,64,128]{2,1,0:T(8,128)(2,1)S(1)} %all-to-all-done.1.msg_ref, f32[1,64,64]{2,1,0:T(8,128)S(1)} %copy-done, f32[1,64,64]{2,1,0:T(8,128)S(1)} %copy-done.1, f32[1280,128]{1,0:T(8,128)S(1)} %get-tuple-element.16.base_ref, ...), custom_call_target="tpu_custom_call" | custom-call | tf_op jit(solution)/shard_map/finish/pallas_call | solution.py:468
  58.9 17.1 %all_to_all.15.x_ref = bf16[32,20,128]{2,1,0:T(8,128)(2,1)S(1)} all-to-all(bf16[32,20,128]{2,1,0:T(8,128)(2,1)S(1)} %finish.1), channel_id=1, replica_groups=mesh['seg'=16,'grp'=32] {'grp'}, dimensions={0} | all-to-all | bytes 327680 | tf_op jit(solution)/shard_map/all_to_all | solution.py:502
  76.0 0.8 %unpack.1 = bf16[40,2048]{1,0:T(8,128)(2,1)} custom-call(bf16[32,20,128]{2,1,0:T(8,128)(2,1)S(1)} %all_to_all.15.x_ref), custom_call_target="tpu_custom_call" | custom-call | tf_op jit(solution)/shard_map/unpack/pallas_call | solution.py:492
Async XLA Ops:
  2.0 29.6 %all-to-all-start = ((bf16[32,64,128]{2,1,0:T(8,128)(2,1)}), bf16[32,64,128]{2,1,0:T(8,128)(2,1)S(1)}, u32[]{:S(2)}, u32[]{:S(2)}) async-start(bf16[32,64,128]{2,1,0:T(8,128)(2,1)} %pack.1), calls=%async_computation | async-start | bytes 1048576 | tf_op jit(solution)/shard_map/all_to_all | solution.py:502
  36.9 20.3 %all-to-all-start.1 = ((bf16[16,64,128]{2,1,0:T(8,128)(2,1)}), bf16[16,64,128]{2,1,0:T(8,128)(2,1)S(1)}, u32[]{:S(2)}, u32[]{:S(2)}) async-start(bf16[16,64,128]{2,1,0:T(8,128)(2,1)} %get-tuple-element.12), calls=%async_computation.1 | async-start | bytes 524288 | tf_op jit(solution)/shard_map/all_to_all | solution.py:502
  46.0 11.2 %copy-start = (f32[1,64,64]{2,1,0:T(8,128)S(1)}, f32[1,64,64]{2,1,0:T(8,128)}, u32[]{:S(2)}) copy-start(f32[1,64,64]{2,1,0:T(8,128)} %sf_ref.1) | copy-start | bytes 49156
  46.0 11.2 %copy-start.1 = (f32[1,64,64]{2,1,0:T(8,128)S(1)}, f32[1,64,64]{2,1,0:T(8,128)}, u32[]{:S(2)}) copy-start(f32[1,64,64]{2,1,0:T(8,128)} %sb_ref.1) | copy-start | bytes 49156

commit v4 on v3

--- a/solution.py
+++ b/solution.py
@@ -152,7 +152,7 @@
 
 def attend_body(
     tv_ref, me_ref, recv_ref, msg_ref, qk_ref, ar_ref, g_ref,
-    qk_scr, v_scr, r_scr, inv_scr, rate_scr, k2_scr, qs_scr, tf_scr, tb_scr, da_scr, ckh_scr, ckl_scr, h_scr,
+    qk_scr, v_scr, r_scr, inv_scr, rate_scr, k2_scr, qs_scr, tf_scr, tb_scr, da_scr, ckh_scr, ckl_scr, h_scr, reach_scr,
 ):
     groups, rows, _ = recv_ref.shape
     toks = rows - 24
@@ -248,9 +248,16 @@
         scores = mm_nt(qs_scr[AROWS * b : AROWS * (b + 1)], k2_scr[...])
         return jnp.concatenate([jnp.where(cols < valid, scores[:, 0:TEXT], -1e30), scores[:, TEXT:]], axis=1)
 
+    def close(b, raised, row_total):
+        at = slice(AROWS * b, AROWS * (b + 1))
+        att = (mm(raised, v2) / row_total).astype(bf16).astype(f32)
+        ar_ref[at] = jnp.where(left_part, att, rate_scr[at]).astype(bf16)
+        da_scr[at] = packed(inv_scr[at] * att)
+
     scores = scores_of(0)
     for b in range(parts):
-        at = slice(AROWS * b, AROWS * (b + 1))
+        if b:
+            close(b - 1, raised, row_total)
         following = scores_of(b + 1) if b + 1 < parts else None
         for m in range(chunks // 2 * b // parts, chunks // 2 * (b + 1) // parts):
             t_f = advance_f(t_f, m)
@@ -258,20 +265,15 @@
         peak = jnp.max(scores, axis=1, keepdims=True)
         raised = jnp.exp(scores - peak)
         row_total = jnp.sum(raised, axis=1, keepdims=True)
-        att = (mm(raised.astype(bf16), v2) / row_total).astype(bf16).astype(f32)
-        ar_ref[at] = jnp.where(left_part, att, rate_scr[at]).astype(bf16)
-        da_scr[at] = packed(inv_scr[at] * att)
+        raised = raised.astype(bf16)
         scores = following
-
-    total = jnp.zeros((LANES, 2 * LANES), f32)
-    for b in range(blocks):
-        reach = []
-        for n in range(QROWS // GROUP * b, QROWS // GROUP * (b + 1)):
-            at = slice(GROUP * n, GROUP * (n + 1))
-            hi, lo = split(mm_nt(k2_scr[at], jnp.concatenate([tf_scr[at], tb_scr[at]], axis=0)))
-            reach.append(jnp.concatenate([hi, lo], axis=1))
-        at = slice(QROWS * b, QROWS * (b + 1))
-        total = total + mm_tn(da_scr[at], jnp.concatenate(reach, axis=0))
+    close(parts - 1, raised, row_total)
+
+    for n in range(chunks):
+        at = slice(GROUP * n, GROUP * (n + 1))
+        hi, lo = split(mm_nt(k2_scr[at], jnp.concatenate([tf_scr[at], tb_scr[at]], axis=0)))
+        reach_scr[at] = jnp.concatenate([hi, lo], axis=1)
+    total = mm_tn(da_scr[...], reach_scr[...])
     total = total[0:HDIM] + total[HDIM : 2 * HDIM]
     shift_f = total[:, 0:LANES] + total[:, LANES : 2 * LANES]
     shift_b = swap_halves(shift_f)
@@ -298,6 +300,7 @@
         + [jax.ShapeDtypeStruct((chunks, LANES, LANES), bf16)],
         scratch_shapes=[
             *[pltpu.VMEM(tall, f32)] * 5, *[pltpu.VMEM(tall, bf16)] * 7, pltpu.VMEM((chunks // 2, LANES, LANES), bf16),
+            pltpu.VMEM((seglen, 2 * LANES), bf16),
         ],
         compiler_params=pltpu.CompilerParams(vmem_limit_bytes=VMEM_LIMIT),
         name="attend",
@@ -425,12 +428,16 @@
     def times(x, decay):
         return mm(twice(packed(x)), four(*split(decay)))
 
+    def times_sent(x, decay):
+        decay = decay.astype(bf16)
+        return mm(packed(x), jnp.concatenate([decay, decay], axis=0))
+
     def leaf(i):
         m = msg_ref[i].astype(f32)
         m_sw = swap_halves(m)
         return jnp.concatenate([jnp.where(left64, m, m_sw), jnp.where(left64, m_sw, m)], axis=0)
 
-    def then(first, second):
+    def then(first, second, times):
         return first + second + times(first, second[0:HDIM])
 
     def sibling(level):
@@ -439,14 +446,16 @@
         before = lax.rem(block, 2) == 1
         start = jnp.where(before, block - 1, block + 1) * size
         nodes = [leaf(start + jnp.where(before, i, size - 1 - i)) for i in range(size)]
+        way = times_sent
         while len(nodes) > 1:
-            nodes = [then(nodes[i], nodes[i + 1]) for i in range(0, len(nodes), 2)]
-        return before, nodes[0]
+            nodes = [then(nodes[i], nodes[i + 1], way) for i in range(0, len(nodes), 2)]
+            way = times
+        return before, nodes[0], way
 
     w_f, w_b = doubled_transpose(sf_ref[0]), doubled_transpose(sb_ref[0])
-    for before, node in [sibling(level) for level in reversed(range(segments.bit_length() - 1))]:
+    for before, node, way in [sibling(level) for level in reversed(range(segments.bit_length() - 1))]:
         state = jnp.where(before, w_f, w_b)
-        state = state + times(state, node[0:HDIM]) + node[HDIM : 2 * HDIM]
+        state = state + way(state, node[0:HDIM]) + node[HDIM : 2 * HDIM]
         w_f, w_b = jnp.where(before, state, w_f), jnp.where(before, w_b, state)
     w_hi, w_lo = split(jnp.where(left64, w_f, w_b))
     w_row = jnp.concatenate([w_hi, w_hi, w_lo], axis=1)

time: 77.3 us -> 76.9 us (level)
  no operation moved by 1% of the time
where the time goes in v4:
time: 76.9 us; the launch traced here: 76.4 us
  starting transfers between devices  22 us (29%)
  waiting for transfers between devices  21.7 us (28%)
  blocking collectives  17.1 us (22%)
  Pallas kernels  14.9 us (19%)
    all_to_all x2, starting transfers between devices, exchange(): return lax.all_to_all(x, axis, split_axis=0, concat_axis=0, tiled=True)  22 us
    all_to_all x2, waiting for transfers between devices, exchange(): return lax.all_to_all(x, axis, split_axis=0, concat_axis=0, tiled=True)  21.7 us
    all_to_all x1, blocking collectives, exchange(): return lax.all_to_all(x, axis, split_axis=0, concat_axis=0, tiled=True)  17.1 us
    pallas_call x1, Pallas kernels, operators(): pl.pallas_call(operators_body, out_shape=[jax.ShapeDtypeStruct(tall, f32)...  5.58 us
    pallas_call x1, Pallas kernels, attend(): pl.pallas_call(attend_body, in_specs=[smem, smem, vmem], out_specs=[vmem]...  4.91 us
    pallas_call x1, Pallas kernels, pack(): pl.pallas_call(pack_body, in_specs=[pl.BlockSpec(memory_space=pl.ANY)] *...  2.04 us
    pallas_call x1, Pallas kernels, finish(): pl.pallas_call(finish_body, in_specs=[smem] + [vmem] * 6, out_specs=vmem,...  1.56 us
  transfers between devices with their start and end apart: 2, of which 2 were waited for; matrix products, arithmetic and copies ran while one was open for 0% of the time, Pallas kernels for 7%

profile of v4, /device:TPU:1, one launch (start us, length us, event | category | flops | bytes accessed | tf_op | source)
XLA Modules:
  0.0 76.4 jit_solution(10347520165494658749)
XLA Ops:
  0.0 2.0 %pack.1 = bf16[32,64,128]{2,1,0:T(8,128)(2,1)} custom-call(bf16[40,2048]{1,0:T(8,128)(2,1)} %q_hbm.1, bf16[40,2048]{1,0:T(8,128)(2,1)} %k_hbm.1, bf16[40,2048]{1,0:T(8,128)(2,1)} %v_hbm.1, bf16[32,40]{1,0:T(8,128)(2,1)} %bitcast.2), custom_call_target="tpu_custom_call" | custom-call | tf_op jit(solution)/shard_map/pack/pallas_call | solution.py:102
  2.0 12.9 %all-to-all-start = ((bf16[32,64,128]{2,1,0:T(8,128)(2,1)}), bf16[32,64,128]{2,1,0:T(8,128)(2,1)S(1)}, u32[]{:S(2)}, u32[]{:S(2)}) async-start(bf16[32,64,128]{2,1,0:T(8,128)(2,1)} %pack.1), calls=%async_computation | async-start | bytes 1048576 | tf_op jit(solution)/shard_map/all_to_all | solution.py:511
  15.6 16.1 %all-to-all-done.recv_ref = bf16[32,64,128]{2,1,0:T(8,128)(2,1)S(1)} async-done(((bf16[32,64,128]{2,1,0:T(8,128)(2,1)}), bf16[32,64,128]{2,1,0:T(8,128)(2,1)S(1)}, u32[]{:S(2)}, u32[]{:S(2)}) %all-to-all-start) | async-done | bytes 524320 | tf_op jit(solution)/shard_map/all_to_all | solution.py:511
  31.7 4.9 %attend.1 = (bf16[16,64,128]{2,1,0:T(8,128)(2,1)}, bf16[1280,128]{1,0:T(8,128)(2,1)S(1)}, bf16[1280,128]{1,0:T(8,128)(2,1)S(1)}, bf16[20,128,128]{2,1,0:T(8,128)(2,1)S(1)}) custom-call(s32[1]{0:T(128)S(6)} %copy.8.tv_ref, s32[1]{0:T(128)} %bitcast.me_ref, bf16[32,64,128]{2,1,0:T(8,128)(2,1)S(1)} %all-to-all-done.recv_ref), custom_call_target="tpu_custom_call" | custom-call | tf_op jit(solution)/shard_map/attend/pallas_call | solution.py:294
  36.6 9.1 %all-to-all-start.1 = ((bf16[16,64,128]{2,1,0:T(8,128)(2,1)}), bf16[16,64,128]{2,1,0:T(8,128)(2,1)S(1)}, u32[]{:S(2)}, u32[]{:S(2)}) async-start(bf16[16,64,128]{2,1,0:T(8,128)(2,1)} %get-tuple-element.12), calls=%async_computation.1 | async-start | bytes 524288 | tf_op jit(solution)/shard_map/all_to_all | solution.py:511
  45.7 0.0 copy-start
  45.7 0.0 copy-start.1
  45.7 5.6 %operators.1 = (f32[1280,128]{1,0:T(8,128)S(1)}, bf16[1280,128]{1,0:T(8,128)(2,1)S(1)}, bf16[1280,128]{1,0:T(8,128)(2,1)S(1)}) custom-call(bf16[1280,128]{1,0:T(8,128)(2,1)S(1)} %get-tuple-element.13.qk_ref, bf16[1280,128]{1,0:T(8,128)(2,1)S(1)} %get-tuple-element.14.ar_ref, bf16[20,128,128]{2,1,0:T(8,128)(2,1)S(1)} %get-tuple-element.15.g_ref), custom_call_target="tpu_custom_call" | custom-call | flops 2000000000 | bytes 8000000 | tf_op jit(solution)/shard_map/operators/pallas_call | solution.py:400
  51.3 5.6 %all-to-all-done.1.msg_ref = bf16[16,64,128]{2,1,0:T(8,128)(2,1)S(1)} async-done(((bf16[16,64,128]{2,1,0:T(8,128)(2,1)}), bf16[16,64,128]{2,1,0:T(8,128)(2,1)S(1)}, u32[]{:S(2)}, u32[]{:S(2)}) %all-to-all-start.1) | async-done | bytes 262176 | tf_op jit(solution)/shard_map/all_to_all | solution.py:511
  56.9 0.0 copy-done
  56.9 0.0 copy-done.1
  56.9 1.6 %finish.1 = bf16[32,20,128]{2,1,0:T(8,128)(2,1)S(1)} custom-call(s32[1]{0:T(128)} %bitcast.me_ref, bf16[16,64,128]{2,1,0:T(8,128)(2,1)S(1)} %all-to-all-done.1.msg_ref, f32[1,64,64]{2,1,0:T(8,128)S(1)} %copy-done, f32[1,64,64]{2,1,0:T(8,128)S(1)} %copy-done.1, f32[1280,128]{1,0:T(8,128)S(1)} %get-tuple-element.16.base_ref, ...), custom_call_target="tpu_custom_call" | custom-call | tf_op jit(solution)/shard_map/finish/pallas_call | solution.py:477
  58.5 17.1 %all_to_all.15.x_ref = bf16[32,20,128]{2,1,0:T(8,128)(2,1)S(1)} all-to-all(bf16[32,20,128]{2,1,0:T(8,128)(2,1)S(1)} %finish.1), channel_id=1, replica_groups=mesh['seg'=16,'grp'=32] {'grp'}, dimensions={0} | all-to-all | bytes 327680 | tf_op jit(solution)/shard_map/all_to_all | solution.py:511
  75.6 0.8 %unpack.1 = bf16[40,2048]{1,0:T(8,128)(2,1)} custom-call(bf16[32,20,128]{2,1,0:T(8,128)(2,1)S(1)} %all_to_all.15.x_ref), custom_call_target="tpu_custom_call" | custom-call | tf_op jit(solution)/shard_map/unpack/pallas_call | solution.py:501
Async XLA Ops:
  2.0 29.6 %all-to-all-start = ((bf16[32,64,128]{2,1,0:T(8,128)(2,1)}), bf16[32,64,128]{2,1,0:T(8,128)(2,1)S(1)}, u32[]{:S(2)}, u32[]{:S(2)}) async-start(bf16[32,64,128]{2,1,0:T(8,128)(2,1)} %pack.1), calls=%async_computation | async-start | bytes 1048576 | tf_op jit(solution)/shard_map/all_to_all | solution.py:511
  36.6 20.3 %all-to-all-start.1 = ((bf16[16,64,128]{2,1,0:T(8,128)(2,1)}), bf16[16,64,128]{2,1,0:T(8,128)(2,1)S(1)}, u32[]{:S(2)}, u32[]{:S(2)}) async-start(bf16[16,64,128]{2,1,0:T(8,128)(2,1)} %get-tuple-element.12), calls=%async_computation.1 | async-start | bytes 524288 | tf_op jit(solution)/shard_map/all_to_all | solution.py:511
  45.7 11.2 %copy-start = (f32[1,64,64]{2,1,0:T(8,128)S(1)}, f32[1,64,64]{2,1,0:T(8,128)}, u32[]{:S(2)}) copy-start(f32[1,64,64]{2,1,0:T(8,128)} %sf_ref.1) | copy-start | bytes 49156
  45.7 11.2 %copy-start.1 = (f32[1,64,64]{2,1,0:T(8,128)S(1)}, f32[1,64,64]{2,1,0:T(8,128)}, u32[]{:S(2)}) copy-start(f32[1,64,64]{2,1,0:T(8,128)} %sb_ref.1) | copy-start | bytes 49156

commit v5 on v4

--- a/solution.py
+++ b/solution.py
@@ -13,6 +13,7 @@
 LANES = 128
 QROWS = 256
 AROWS = 128
+QUAD = 4
 PACK_PARTS = 2
 VMEM_LIMIT = 24 * 1024 * 1024
 PACK_LIMIT = 62 * 1024 * 1024
@@ -416,9 +417,10 @@
     )(*held)
 
 
-def finish_body(me_ref, msg_ref, sf_ref, sb_ref, base_ref, ehi_ref, elo_ref, out_ref, scr):
+def finish_body(me_ref, msg_ref, sf_ref, sb_ref, base_ref, ehi_ref, elo_ref, out_ref):
     segments = msg_ref.shape[0]
-    groups, half, _ = out_ref.shape
+    groups, quad, wide = out_ref.shape
+    half = quad * wide // LANES
     me = me_ref[0]
     left64 = lanes_left(HDIM)
 
@@ -461,12 +463,14 @@
     w_row = jnp.concatenate([w_hi, w_hi, w_lo], axis=1)
     e_hi = ehi_ref[...]
     got = mm_nt(jnp.concatenate([e_hi, elo_ref[...], e_hi], axis=1), jnp.concatenate([w_row, w_row], axis=0))
-    scr[...] = got + base_ref[...]
-    left = lanes_left(half)
+    whole = got + base_ref[...]
+    left = lanes_left(2 * quad)
     for g in range(groups):
-        first = scr[2 * half * g : 2 * half * g + half]
-        second = scr[2 * half * g + half : 2 * half * (g + 1)]
-        out_ref[g] = jnp.where(left, first, second).astype(bf16)
+        for j in range(wide // LANES):
+            row = 2 * half * g + 2 * quad * j
+            rows = whole[row : row + 2 * quad]
+            both = jnp.where(left, rows, pltpu.roll(rows, quad, 0))
+            out_ref[g, :, LANES * j : LANES * (j + 1)] = both[0:quad].astype(bf16)
 
 
 def finish(me, maps, state_fwd, state_bwd, base, ehi, elo, groups):
@@ -478,30 +482,38 @@
         finish_body,
         in_specs=[smem] + [vmem] * 6,
         out_specs=vmem,
-        out_shape=jax.ShapeDtypeStruct((groups, half, LANES), bf16),
-        scratch_shapes=[pltpu.VMEM((seglen, LANES), f32)],
+        out_shape=jax.ShapeDtypeStruct((groups, QUAD, half // QUAD * LANES), bf16),
         compiler_params=pltpu.CompilerParams(vmem_limit_bytes=VMEM_LIMIT),
         name="finish",
     )(me, maps, state_fwd, state_bwd, base, ehi, elo)
 
 
-def unpack_body(x_ref, out_ref, scr):
-    heads, half, _ = x_ref.shape
+def unpack_body(x_ref, out_ref, scr, rows_scr):
+    heads, quad, wide = x_ref.shape
+    half = quad * wide // LANES
     left = lanes_left(half)
+    for head in range(heads):
+        for j in range(wide // LANES):
+            rows_scr[head, quad * j : quad * (j + 1)] = x_ref[head, :, LANES * j : LANES * (j + 1)].astype(f32)
     for p in range(heads // 2):
-        even = x_ref[2 * p].astype(f32)
-        odd = x_ref[2 * p + 1].astype(f32)
-        scr[0:half] = jnp.where(left, even, swap_halves(odd))
-        scr[half : 2 * half] = jnp.where(left, swap_halves(even), odd)
-        out_ref[:, LANES * p : LANES * (p + 1)] = scr[...].astype(bf16)
+        even = rows_scr[2 * p]
+        odd = rows_scr[2 * p + 1]
+        first = jnp.where(left, even, swap_halves(odd))
+        second = jnp.where(left, swap_halves(even), odd)
+        for j in range(wide // LANES):
+            scr[p, 2 * quad * j : 2 * quad * j + quad] = first[quad * j : quad * (j + 1)]
+            scr[p, 2 * quad * j + quad : 2 * quad * (j + 1)] = second[quad * j : quad * (j + 1)]
+    for p in range(heads // 2):
+        out_ref[:, LANES * p : LANES * (p + 1)] = scr[p].astype(bf16)
 
 
 def unpack(x):
-    heads, half, _ = x.shape
+    heads, quad, wide = x.shape
+    half = quad * wide // LANES
     return pl.pallas_call(
         unpack_body,
         out_shape=jax.ShapeDtypeStruct((2 * half, heads * HDIM), bf16),
-        scratch_shapes=[pltpu.VMEM((2 * half, LANES), f32)],
+        scratch_shapes=[pltpu.VMEM((heads // 2, 2 * half, LANES), f32), pltpu.VMEM((heads, half, LANES), f32)],
         compiler_params=pltpu.CompilerParams(vmem_limit_bytes=VMEM_LIMIT),
         name="unpack",
     )(x)

time: 76.9 us -> 76.4 us (level)
  no operation moved by 1% of the time
where the time goes in v5:
time: 76.4 us; the launch traced here: 75.9 us
  starting transfers between devices  22 us (29%)
  waiting for transfers between devices  21.7 us (28%)
  blocking collectives  16.7 us (22%)
  Pallas kernels  14.8 us (19%)
    all_to_all x2, starting transfers between devices, exchange(): return lax.all_to_all(x, axis, split_axis=0, concat_axis=0, tiled=True)  22 us
    all_to_all x2, waiting for transfers between devices, exchange(): return lax.all_to_all(x, axis, split_axis=0, concat_axis=0, tiled=True)  21.7 us
    all_to_all x1, blocking collectives, exchange(): return lax.all_to_all(x, axis, split_axis=0, concat_axis=0, tiled=True)  16.7 us
    pallas_call x1, Pallas kernels, operators(): pl.pallas_call(operators_body, out_shape=[jax.ShapeDtypeStruct(tall, f32)...  5.58 us
    pallas_call x1, Pallas kernels, attend(): pl.pallas_call(attend_body, in_specs=[smem, smem, vmem], out_specs=[vmem]...  4.91 us
    pallas_call x1, Pallas kernels, pack(): pl.pallas_call(pack_body, in_specs=[pl.BlockSpec(memory_space=pl.ANY)] *...  2.04 us
  transfers between devices with their start and end apart: 2, of which 2 were waited for; matrix products, arithmetic and copies ran while one was open for 0% of the time, Pallas kernels for 7%

profile of v5, /device:TPU:1, one launch (start us, length us, event | category | flops | bytes accessed | tf_op | source)
XLA Modules:
  0.0 75.9 jit_solution(14320457590125700573)
XLA Ops:
  0.0 2.0 %pack.1 = bf16[32,64,128]{2,1,0:T(8,128)(2,1)} custom-call(bf16[40,2048]{1,0:T(8,128)(2,1)} %q_hbm.1, bf16[40,2048]{1,0:T(8,128)(2,1)} %k_hbm.1, bf16[40,2048]{1,0:T(8,128)(2,1)} %v_hbm.1, bf16[32,40]{1,0:T(8,128)(2,1)} %bitcast.2), custom_call_target="tpu_custom_call" | custom-call | tf_op jit(solution)/shard_map/pack/pallas_call | solution.py:103
  2.0 12.9 %all-to-all-start = ((bf16[32,64,128]{2,1,0:T(8,128)(2,1)}), bf16[32,64,128]{2,1,0:T(8,128)(2,1)S(1)}, u32[]{:S(2)}, u32[]{:S(2)}) async-start(bf16[32,64,128]{2,1,0:T(8,128)(2,1)} %pack.1), calls=%async_computation | async-start | bytes 1048576 | tf_op jit(solution)/shard_map/all_to_all | solution.py:523
  15.6 16.1 %all-to-all-done.recv_ref = bf16[32,64,128]{2,1,0:T(8,128)(2,1)S(1)} async-done(((bf16[32,64,128]{2,1,0:T(8,128)(2,1)}), bf16[32,64,128]{2,1,0:T(8,128)(2,1)S(1)}, u32[]{:S(2)}, u32[]{:S(2)}) %all-to-all-start) | async-done | bytes 524320 | tf_op jit(solution)/shard_map/all_to_all | solution.py:523
  31.7 4.9 %attend.1 = (bf16[16,64,128]{2,1,0:T(8,128)(2,1)}, bf16[1280,128]{1,0:T(8,128)(2,1)S(1)}, bf16[1280,128]{1,0:T(8,128)(2,1)S(1)}, bf16[20,128,128]{2,1,0:T(8,128)(2,1)S(1)}) custom-call(s32[1]{0:T(128)S(6)} %copy.8.tv_ref, s32[1]{0:T(128)} %bitcast.me_ref, bf16[32,64,128]{2,1,0:T(8,128)(2,1)S(1)} %all-to-all-done.recv_ref), custom_call_target="tpu_custom_call" | custom-call | tf_op jit(solution)/shard_map/attend/pallas_call | solution.py:295
  36.6 9.1 %all-to-all-start.1 = ((bf16[16,64,128]{2,1,0:T(8,128)(2,1)}), bf16[16,64,128]{2,1,0:T(8,128)(2,1)S(1)}, u32[]{:S(2)}, u32[]{:S(2)}) async-start(bf16[16,64,128]{2,1,0:T(8,128)(2,1)} %get-tuple-element.12), calls=%async_computation.1 | async-start | bytes 524288 | tf_op jit(solution)/shard_map/all_to_all | solution.py:523
  45.7 0.0 copy-start
  45.7 0.0 copy-start.1
  45.7 5.6 %operators.1 = (f32[1280,128]{1,0:T(8,128)S(1)}, bf16[1280,128]{1,0:T(8,128)(2,1)S(1)}, bf16[1280,128]{1,0:T(8,128)(2,1)S(1)}) custom-call(bf16[1280,128]{1,0:T(8,128)(2,1)S(1)} %get-tuple-element.13.qk_ref, bf16[1280,128]{1,0:T(8,128)(2,1)S(1)} %get-tuple-element.14.ar_ref, bf16[20,128,128]{2,1,0:T(8,128)(2,1)S(1)} %get-tuple-element.15.g_ref), custom_call_target="tpu_custom_call" | custom-call | flops 2000000000 | bytes 8000000 | tf_op jit(solution)/shard_map/operators/pallas_call | solution.py:401
  51.3 5.6 %all-to-all-done.1.msg_ref = bf16[16,64,128]{2,1,0:T(8,128)(2,1)S(1)} async-done(((bf16[16,64,128]{2,1,0:T(8,128)(2,1)}), bf16[16,64,128]{2,1,0:T(8,128)(2,1)S(1)}, u32[]{:S(2)}, u32[]{:S(2)}) %all-to-all-start.1) | async-done | bytes 262176 | tf_op jit(solution)/shard_map/all_to_all | solution.py:523
  56.9 0.0 copy-done
  56.9 0.0 copy-done.1
  56.9 1.5 %finish.1 = bf16[32,4,640]{2,1,0:T(4,128)(2,1)S(1)} custom-call(s32[1]{0:T(128)} %bitcast.me_ref, bf16[16,64,128]{2,1,0:T(8,128)(2,1)S(1)} %all-to-all-done.1.msg_ref, f32[1,64,64]{2,1,0:T(8,128)S(1)} %copy-done, f32[1,64,64]{2,1,0:T(8,128)S(1)} %copy-done.1, f32[1280,128]{1,0:T(8,128)S(1)} %get-tuple-element.16.base_ref, ...), custom_call_target="tpu_custom_call" | custom-call | tf_op jit(solution)/shard_map/finish/pallas_call | solution.py:481
  58.4 16.7 %all_to_all.15.x_ref = bf16[32,4,640]{2,1,0:T(4,128)(2,1)S(1)} all-to-all(bf16[32,4,640]{2,1,0:T(4,128)(2,1)S(1)} %finish.1), channel_id=1, replica_groups=mesh['seg'=16,'grp'=32] {'grp'}, dimensions={0} | all-to-all | bytes 327680 | tf_op jit(solution)/shard_map/all_to_all | solution.py:523
  75.1 0.8 %unpack.1 = bf16[40,2048]{1,0:T(8,128)(2,1)} custom-call(bf16[32,4,640]{2,1,0:T(4,128)(2,1)S(1)} %all_to_all.15.x_ref), custom_call_target="tpu_custom_call" | custom-call | tf_op jit(solution)/shard_map/unpack/pallas_call | solution.py:513
Async XLA Ops:
  2.0 29.6 %all-to-all-start = ((bf16[32,64,128]{2,1,0:T(8,128)(2,1)}), bf16[32,64,128]{2,1,0:T(8,128)(2,1)S(1)}, u32[]{:S(2)}, u32[]{:S(2)}) async-start(bf16[32,64,128]{2,1,0:T(8,128)(2,1)} %pack.1), calls=%async_computation | async-start | bytes 1048576 | tf_op jit(solution)/shard_map/all_to_all | solution.py:523
  36.6 20.3 %all-to-all-start.1 = ((bf16[16,64,128]{2,1,0:T(8,128)(2,1)}), bf16[16,64,128]{2,1,0:T(8,128)(2,1)S(1)}, u32[]{:S(2)}, u32[]{:S(2)}) async-start(bf16[16,64,128]{2,1,0:T(8,128)(2,1)} %get-tuple-element.12), calls=%async_computation.1 | async-start | bytes 524288 | tf_op jit(solution)/shard_map/all_to_all | solution.py:523
  45.7 11.2 %copy-start = (f32[1,64,64]{2,1,0:T(8,128)S(1)}, f32[1,64,64]{2,1,0:T(8,128)}, u32[]{:S(2)}) copy-start(f32[1,64,64]{2,1,0:T(8,128)} %sf_ref.1) | copy-start | bytes 49156
  45.7 11.2 %copy-start.1 = (f32[1,64,64]{2,1,0:T(8,128)S(1)}, f32[1,64,64]{2,1,0:T(8,128)}, u32[]{:S(2)}) copy-start(f32[1,64,64]{2,1,0:T(8,128)} %sb_ref.1) | copy-start | bytes 49156

commit v6 on v5

--- a/solution.py
+++ b/solution.py
@@ -89,10 +89,11 @@
                 low = jnp.concatenate([v_left[24:rows], rate], axis=0)
                 vr = jnp.where(left24, low, v_right[0:24])
                 o_ref[head] = jnp.concatenate([qk, vr], axis=0).astype(bf16)
-        own = pl.ds(each * part, each)
-        write = pltpu.make_async_copy(o_ref.at[own], o_hbm.at[own], out_sems.at[part])
-        write.start()
-        writes.append(write)
+            if p % 4 == 3:
+                own = pl.ds(2 * p - 6, 8)
+                write = pltpu.make_async_copy(o_ref.at[own], o_hbm.at[own], out_sems.at[p // 4])
+                write.start()
+                writes.append(write)
     for write in writes:
         write.wait()
 
@@ -113,7 +114,7 @@
             pltpu.VMEM((heads, rows + 24, LANES), bf16),
             pltpu.VMEM((heads, LANES), f32),
             pltpu.SemaphoreType.DMA((PACK_PARTS, 4)),
-            pltpu.SemaphoreType.DMA((PACK_PARTS,)),
+            pltpu.SemaphoreType.DMA((heads // 8,)),
         ],
         compiler_params=pltpu.CompilerParams(vmem_limit_bytes=PACK_LIMIT),
         name="pack",
@@ -255,14 +256,26 @@
         ar_ref[at] = jnp.where(left_part, att, rate_scr[at]).astype(bf16)
         da_scr[at] = packed(inv_scr[at] * att)
 
+    def reach(n):
+        at = slice(GROUP * n, GROUP * (n + 1))
+        hi, lo = split(mm_nt(k2_scr[at], jnp.concatenate([tf_scr[at], tb_scr[at]], axis=0)))
+        reach_scr[at] = jnp.concatenate([hi, lo], axis=1)
+
     scores = scores_of(0)
+    for m in range(2):
+        t_f = advance_f(t_f, m)
+        t_b = advance_b(t_b, chunks // 2 - 1 - m)
     for b in range(parts):
         if b:
             close(b - 1, raised, row_total)
         following = scores_of(b + 1) if b + 1 < parts else None
-        for m in range(chunks // 2 * b // parts, chunks // 2 * (b + 1) // parts):
-            t_f = advance_f(t_f, m)
-            t_b = advance_b(t_b, chunks // 2 - 1 - m)
+        if b + 2 < chunks // 2:
+            t_f = advance_f(t_f, b + 2)
+            t_b = advance_b(t_b, chunks // 2 - 1 - b - 2)
+        else:
+            own = 10 * (b + 2 - chunks // 2)
+            for n in range(own, own + 10):
+                reach(n)
         peak = jnp.max(scores, axis=1, keepdims=True)
         raised = jnp.exp(scores - peak)
         row_total = jnp.sum(raised, axis=1, keepdims=True)
@@ -270,10 +283,6 @@
         scores = following
     close(parts - 1, raised, row_total)
 
-    for n in range(chunks):
-        at = slice(GROUP * n, GROUP * (n + 1))
-        hi, lo = split(mm_nt(k2_scr[at], jnp.concatenate([tf_scr[at], tb_scr[at]], axis=0)))
-        reach_scr[at] = jnp.concatenate([hi, lo], axis=1)
     total = mm_tn(da_scr[...], reach_scr[...])
     total = total[0:HDIM] + total[HDIM : 2 * HDIM]
     shift_f = total[:, 0:LANES] + total[:, LANES : 2 * LANES]
@@ -488,7 +497,7 @@
     )(me, maps, state_fwd, state_bwd, base, ehi, elo)
 
 
-def unpack_body(x_ref, out_ref, scr, rows_scr):
+def unpack_body(x_ref, out_ref, scr, rows_scr, out_scr, sems):
     heads, quad, wide = x_ref.shape
     half = quad * wide // LANES
     left = lanes_left(half)
@@ -503,8 +512,17 @@
         for j in range(wide // LANES):
             scr[p, 2 * quad * j : 2 * quad * j + quad] = first[quad * j : quad * (j + 1)]
             scr[p, 2 * quad * j + quad : 2 * quad * (j + 1)] = second[quad * j : quad * (j + 1)]
-    for p in range(heads // 2):
-        out_ref[:, LANES * p : LANES * (p + 1)] = scr[p].astype(bf16)
+    writes = []
+    parts = sems.shape[0]
+    each = heads // 2 // parts
+    for part in range(parts):
+        for p in range(each * part, each * (part + 1)):
+            out_scr[:, LANES * p : LANES * (p + 1)] = scr[p].astype(bf16)
+        cols = pl.ds(LANES * each * part, LANES * each)
+        writes.append(pltpu.make_async_copy(out_scr.at[:, cols], out_ref.at[:, cols], sems.at[part]))
+        writes[part].start()
+    for write in writes:
+        write.wait()
 
 
 def unpack(x):
@@ -512,8 +530,12 @@
     half = quad * wide // LANES
     return pl.pallas_call(
         unpack_body,
+        out_specs=pl.BlockSpec(memory_space=pl.ANY),
         out_shape=jax.ShapeDtypeStruct((2 * half, heads * HDIM), bf16),
-        scratch_shapes=[pltpu.VMEM((heads // 2, 2 * half, LANES), f32), pltpu.VMEM((heads, half, LANES), f32)],
+        scratch_shapes=[
+            pltpu.VMEM((heads // 2, 2 * half, LANES), f32), pltpu.VMEM((heads, half, LANES), f32),
+            pltpu.VMEM((2 * half, heads * HDIM), bf16), pltpu.SemaphoreType.DMA((2,)),
+        ],
         compiler_params=pltpu.CompilerParams(vmem_limit_bytes=VMEM_LIMIT),
         name="unpack",
     )(x)

time: 76.4 us -> 76.4 us (level)
  no operation moved by 1% of the time
where the time goes in v6:
time: 76.4 us; the launch traced here: 75.9 us
  starting transfers between devices  22 us (29%)
  waiting for transfers between devices  21.7 us (28%)
  blocking collectives  16.6 us (22%)
  Pallas kernels  14.9 us (20%)
    all_to_all x2, starting transfers between devices, exchange(): return lax.all_to_all(x, axis, split_axis=0, concat_axis=0, tiled=True)  22 us
    all_to_all x2, waiting for transfers between devices, exchange(): return lax.all_to_all(x, axis, split_axis=0, concat_axis=0, tiled=True)  21.7 us
    all_to_all x1, blocking collectives, exchange(): return lax.all_to_all(x, axis, split_axis=0, concat_axis=0, tiled=True)  16.6 us
    pallas_call x1, Pallas kernels, operators(): pl.pallas_call(operators_body, out_shape=[jax.ShapeDtypeStruct(tall, f32)...  5.58 us
    pallas_call x1, Pallas kernels, attend(): pl.pallas_call(attend_body, in_specs=[smem, smem, vmem], out_specs=[vmem]...  4.96 us
    pallas_call x1, Pallas kernels, pack(): pl.pallas_call(pack_body, in_specs=[pl.BlockSpec(memory_space=pl.ANY)] *...  2.03 us
  transfers between devices with their start and end apart: 2, of which 2 were waited for; matrix products, arithmetic and copies ran while one was open for 0% of the time, Pallas kernels for 7%

profile of v6, /device:TPU:1, one launch (start us, length us, event | category | flops | bytes accessed | tf_op | source)
XLA Modules:
  0.0 75.9 jit_solution(7682159204531689629)
XLA Ops:
  0.0 2.0 %pack.1 = bf16[32,64,128]{2,1,0:T(8,128)(2,1)} custom-call(bf16[40,2048]{1,0:T(8,128)(2,1)} %q_hbm.1, bf16[40,2048]{1,0:T(8,128)(2,1)} %k_hbm.1, bf16[40,2048]{1,0:T(8,128)(2,1)} %v_hbm.1, bf16[32,40]{1,0:T(8,128)(2,1)} %bitcast.2), custom_call_target="tpu_custom_call" | custom-call | tf_op jit(solution)/shard_map/pack/pallas_call | solution.py:104
  2.0 12.9 %all-to-all-start = ((bf16[32,64,128]{2,1,0:T(8,128)(2,1)}), bf16[32,64,128]{2,1,0:T(8,128)(2,1)S(1)}, u32[]{:S(2)}, u32[]{:S(2)}) async-start(bf16[32,64,128]{2,1,0:T(8,128)(2,1)} %pack.1), calls=%async_computation | async-start | bytes 1048576 | tf_op jit(solution)/shard_map/all_to_all | solution.py:545
  15.6 16.1 %all-to-all-done.recv_ref = bf16[32,64,128]{2,1,0:T(8,128)(2,1)S(1)} async-done(((bf16[32,64,128]{2,1,0:T(8,128)(2,1)}), bf16[32,64,128]{2,1,0:T(8,128)(2,1)S(1)}, u32[]{:S(2)}, u32[]{:S(2)}) %all-to-all-start) | async-done | bytes 524320 | tf_op jit(solution)/shard_map/all_to_all | solution.py:545
  31.7 5.0 %attend.1 = (bf16[16,64,128]{2,1,0:T(8,128)(2,1)}, bf16[1280,128]{1,0:T(8,128)(2,1)S(1)}, bf16[1280,128]{1,0:T(8,128)(2,1)S(1)}, bf16[20,128,128]{2,1,0:T(8,128)(2,1)S(1)}) custom-call(s32[1]{0:T(128)S(6)} %copy.8.tv_ref, s32[1]{0:T(128)} %bitcast.me_ref, bf16[32,64,128]{2,1,0:T(8,128)(2,1)S(1)} %all-to-all-done.recv_ref), custom_call_target="tpu_custom_call" | custom-call | tf_op jit(solution)/shard_map/attend/pallas_call | solution.py:304
  36.6 9.1 %all-to-all-start.1 = ((bf16[16,64,128]{2,1,0:T(8,128)(2,1)}), bf16[16,64,128]{2,1,0:T(8,128)(2,1)S(1)}, u32[]{:S(2)}, u32[]{:S(2)}) async-start(bf16[16,64,128]{2,1,0:T(8,128)(2,1)} %get-tuple-element.12), calls=%async_computation.1 | async-start | bytes 524288 | tf_op jit(solution)/shard_map/all_to_all | solution.py:545
  45.7 0.0 copy-start
  45.7 0.0 copy-start.1
  45.8 5.6 %operators.1 = (f32[1280,128]{1,0:T(8,128)S(1)}, bf16[1280,128]{1,0:T(8,128)(2,1)S(1)}, bf16[1280,128]{1,0:T(8,128)(2,1)S(1)}) custom-call(bf16[1280,128]{1,0:T(8,128)(2,1)S(1)} %get-tuple-element.13.qk_ref, bf16[1280,128]{1,0:T(8,128)(2,1)S(1)} %get-tuple-element.14.ar_ref, bf16[20,128,128]{2,1,0:T(8,128)(2,1)S(1)} %get-tuple-element.15.g_ref), custom_call_target="tpu_custom_call" | custom-call | flops 2000000000 | bytes 8000000 | tf_op jit(solution)/shard_map/operators/pallas_call | solution.py:410
  51.3 5.6 %all-to-all-done.1.msg_ref = bf16[16,64,128]{2,1,0:T(8,128)(2,1)S(1)} async-done(((bf16[16,64,128]{2,1,0:T(8,128)(2,1)}), bf16[16,64,128]{2,1,0:T(8,128)(2,1)S(1)}, u32[]{:S(2)}, u32[]{:S(2)}) %all-to-all-start.1) | async-done | bytes 262176 | tf_op jit(solution)/shard_map/all_to_all | solution.py:545
  57.0 0.0 copy-done
  57.0 0.0 copy-done.1
  57.0 1.5 %finish.1 = bf16[32,4,640]{2,1,0:T(4,128)(2,1)S(1)} custom-call(s32[1]{0:T(128)} %bitcast.me_ref, bf16[16,64,128]{2,1,0:T(8,128)(2,1)S(1)} %all-to-all-done.1.msg_ref, f32[1,64,64]{2,1,0:T(8,128)S(1)} %copy-done, f32[1,64,64]{2,1,0:T(8,128)S(1)} %copy-done.1, f32[1280,128]{1,0:T(8,128)S(1)} %get-tuple-element.16.base_ref, ...), custom_call_target="tpu_custom_call" | custom-call | tf_op jit(solution)/shard_map/finish/pallas_call | solution.py:490
  58.5 16.6 %all_to_all.15.x_ref = bf16[32,4,640]{2,1,0:T(4,128)(2,1)S(1)} all-to-all(bf16[32,4,640]{2,1,0:T(4,128)(2,1)S(1)} %finish.1), channel_id=1, replica_groups=mesh['seg'=16,'grp'=32] {'grp'}, dimensions={0} | all-to-all | bytes 327680 | tf_op jit(solution)/shard_map/all_to_all | solution.py:545
  75.1 0.8 %unpack.1 = bf16[40,2048]{1,0:T(8,128)(2,1)} custom-call(bf16[32,4,640]{2,1,0:T(4,128)(2,1)S(1)} %all_to_all.15.x_ref), custom_call_target="tpu_custom_call" | custom-call | tf_op jit(solution)/shard_map/unpack/pallas_call | solution.py:531
Async XLA Ops:
  2.0 29.6 %all-to-all-start = ((bf16[32,64,128]{2,1,0:T(8,128)(2,1)}), bf16[32,64,128]{2,1,0:T(8,128)(2,1)S(1)}, u32[]{:S(2)}, u32[]{:S(2)}) async-start(bf16[32,64,128]{2,1,0:T(8,128)(2,1)} %pack.1), calls=%async_computation | async-start | bytes 1048576 | tf_op jit(solution)/shard_map/all_to_all | solution.py:545
  36.6 20.3 %all-to-all-start.1 = ((bf16[16,64,128]{2,1,0:T(8,128)(2,1)}), bf16[16,64,128]{2,1,0:T(8,128)(2,1)S(1)}, u32[]{:S(2)}, u32[]{:S(2)}) async-start(bf16[16,64,128]{2,1,0:T(8,128)(2,1)} %get-tuple-element.12), calls=%async_computation.1 | async-start | bytes 524288 | tf_op jit(solution)/shard_map/all_to_all | solution.py:545
  45.7 11.2 %copy-start = (f32[1,64,64]{2,1,0:T(8,128)S(1)}, f32[1,64,64]{2,1,0:T(8,128)}, u32[]{:S(2)}) copy-start(f32[1,64,64]{2,1,0:T(8,128)} %sf_ref.1) | copy-start | bytes 49156
  45.7 11.2 %copy-start.1 = (f32[1,64,64]{2,1,0:T(8,128)S(1)}, f32[1,64,64]{2,1,0:T(8,128)}, u32[]{:S(2)}) copy-start(f32[1,64,64]{2,1,0:T(8,128)} %sb_ref.1) | copy-start | bytes 49156

commit v7 on v5

--- a/solution.py
+++ b/solution.py
@@ -202,6 +202,15 @@
         ck_hi, ck_lo = split(step * inv_k * k2)
         ckh_scr[at] = ck_hi
         ckl_scr[at] = ck_lo
+    parts = seglen // AROWS
+    cols = lax.broadcasted_iota(jnp.int32, (AROWS, TEXT), 1)
+    left_part = lanes_left(AROWS)
+
+    def scores_of(b):
+        scores = mm_nt(qs_scr[AROWS * b : AROWS * (b + 1)], k2_scr[...])
+        return jnp.concatenate([jnp.where(cols < valid, scores[:, 0:TEXT], -1e30), scores[:, TEXT:]], axis=1)
+
+    scores = scores_of(0)
     for n in range(chunks):
         at = slice(GROUP * n, GROUP * (n + 1))
         k = k2_scr[at, 0:HDIM]
@@ -241,21 +250,12 @@
     def keep(ref, n, p):
         ref[GROUP * n : GROUP * (n + 1)] = p
 
-    parts = seglen // AROWS
-    cols = lax.broadcasted_iota(jnp.int32, (AROWS, TEXT), 1)
-    left_part = lanes_left(AROWS)
-
-    def scores_of(b):
-        scores = mm_nt(qs_scr[AROWS * b : AROWS * (b + 1)], k2_scr[...])
-        return jnp.concatenate([jnp.where(cols < valid, scores[:, 0:TEXT], -1e30), scores[:, TEXT:]], axis=1)
-
     def close(b, raised, row_total):
         at = slice(AROWS * b, AROWS * (b + 1))
         att = (mm(raised, v2) / row_total).astype(bf16).astype(f32)
         ar_ref[at] = jnp.where(left_part, att, rate_scr[at]).astype(bf16)
         da_scr[at] = packed(inv_scr[at] * att)
 
-    scores = scores_of(0)
     for b in range(parts):
         if b:
             close(b - 1, raised, row_total)

time: 76.4 us -> 76.4 us (level)
  no operation moved by 1% of the time
where the time goes in v7:
time: 76.4 us; the launch traced here: 76 us
  starting transfers between devices  22 us (29%)
  waiting for transfers between devices  21.7 us (28%)
  blocking collectives  16.6 us (22%)
  Pallas kernels  14.9 us (20%)
    all_to_all x2, starting transfers between devices, exchange(): return lax.all_to_all(x, axis, split_axis=0, concat_axis=0, tiled=True)  22 us
    all_to_all x2, waiting for transfers between devices, exchange(): return lax.all_to_all(x, axis, split_axis=0, concat_axis=0, tiled=True)  21.7 us
    all_to_all x1, blocking collectives, exchange(): return lax.all_to_all(x, axis, split_axis=0, concat_axis=0, tiled=True)  16.6 us
    pallas_call x1, Pallas kernels, operators(): pl.pallas_call(operators_body, out_shape=[jax.ShapeDtypeStruct(tall, f32)...  5.58 us
    pallas_call x1, Pallas kernels, attend(): pl.pallas_call(attend_body, in_specs=[smem, smem, vmem], out_specs=[vmem]...  4.97 us
    pallas_call x1, Pallas kernels, pack(): pl.pallas_call(pack_body, in_specs=[pl.BlockSpec(memory_space=pl.ANY)] *...  2.04 us
  transfers between devices with their start and end apart: 2, of which 2 were waited for; matrix products, arithmetic and copies ran while one was open for 0% of the time, Pallas kernels for 7%

profile of v7, /device:TPU:1, one launch (start us, length us, event | category | flops | bytes accessed | tf_op | source)
XLA Modules:
  0.0 76.0 jit_solution(15240301334526251235)
XLA Ops:
  0.0 2.0 %pack.1 = bf16[32,64,128]{2,1,0:T(8,128)(2,1)} custom-call(bf16[40,2048]{1,0:T(8,128)(2,1)} %q_hbm.1, bf16[40,2048]{1,0:T(8,128)(2,1)} %k_hbm.1, bf16[40,2048]{1,0:T(8,128)(2,1)} %v_hbm.1, bf16[32,40]{1,0:T(8,128)(2,1)} %bitcast.2), custom_call_target="tpu_custom_call" | custom-call | tf_op jit(solution)/shard_map/pack/pallas_call | solution.py:103
  2.0 12.9 %all-to-all-start = ((bf16[32,64,128]{2,1,0:T(8,128)(2,1)}), bf16[32,64,128]{2,1,0:T(8,128)(2,1)S(1)}, u32[]{:S(2)}, u32[]{:S(2)}) async-start(bf16[32,64,128]{2,1,0:T(8,128)(2,1)} %pack.1), calls=%async_computation | async-start | bytes 1048576 | tf_op jit(solution)/shard_map/all_to_all | solution.py:523
  15.6 16.1 %all-to-all-done.recv_ref = bf16[32,64,128]{2,1,0:T(8,128)(2,1)S(1)} async-done(((bf16[32,64,128]{2,1,0:T(8,128)(2,1)}), bf16[32,64,128]{2,1,0:T(8,128)(2,1)S(1)}, u32[]{:S(2)}, u32[]{:S(2)}) %all-to-all-start) | async-done | bytes 524320 | tf_op jit(solution)/shard_map/all_to_all | solution.py:523
  31.7 5.0 %attend.1 = (bf16[16,64,128]{2,1,0:T(8,128)(2,1)}, bf16[1280,128]{1,0:T(8,128)(2,1)S(1)}, bf16[1280,128]{1,0:T(8,128)(2,1)S(1)}, bf16[20,128,128]{2,1,0:T(8,128)(2,1)S(1)}) custom-call(s32[1]{0:T(128)S(6)} %copy.8.tv_ref, s32[1]{0:T(128)} %bitcast.me_ref, bf16[32,64,128]{2,1,0:T(8,128)(2,1)S(1)} %all-to-all-done.recv_ref), custom_call_target="tpu_custom_call" | custom-call | tf_op jit(solution)/shard_map/attend/pallas_call | solution.py:295
  36.7 9.1 %all-to-all-start.1 = ((bf16[16,64,128]{2,1,0:T(8,128)(2,1)}), bf16[16,64,128]{2,1,0:T(8,128)(2,1)S(1)}, u32[]{:S(2)}, u32[]{:S(2)}) async-start(bf16[16,64,128]{2,1,0:T(8,128)(2,1)} %get-tuple-element.12), calls=%async_computation.1 | async-start | bytes 524288 | tf_op jit(solution)/shard_map/all_to_all | solution.py:523
  45.8 0.0 copy-start
  45.8 0.0 copy-start.1
  45.8 5.6 %operators.1 = (f32[1280,128]{1,0:T(8,128)S(1)}, bf16[1280,128]{1,0:T(8,128)(2,1)S(1)}, bf16[1280,128]{1,0:T(8,128)(2,1)S(1)}) custom-call(bf16[1280,128]{1,0:T(8,128)(2,1)S(1)} %get-tuple-element.13.qk_ref, bf16[1280,128]{1,0:T(8,128)(2,1)S(1)} %get-tuple-element.14.ar_ref, bf16[20,128,128]{2,1,0:T(8,128)(2,1)S(1)} %get-tuple-element.15.g_ref), custom_call_target="tpu_custom_call" | custom-call | flops 2000000000 | bytes 8000000 | tf_op jit(solution)/shard_map/operators/pallas_call | solution.py:401
  51.4 5.6 %all-to-all-done.1.msg_ref = bf16[16,64,128]{2,1,0:T(8,128)(2,1)S(1)} async-done(((bf16[16,64,128]{2,1,0:T(8,128)(2,1)}), bf16[16,64,128]{2,1,0:T(8,128)(2,1)S(1)}, u32[]{:S(2)}, u32[]{:S(2)}) %all-to-all-start.1) | async-done | bytes 262176 | tf_op jit(solution)/shard_map/all_to_all | solution.py:523
  57.0 0.0 copy-done
  57.0 0.0 copy-done.1
  57.0 1.5 %finish.1 = bf16[32,4,640]{2,1,0:T(4,128)(2,1)S(1)} custom-call(s32[1]{0:T(128)} %bitcast.me_ref, bf16[16,64,128]{2,1,0:T(8,128)(2,1)S(1)} %all-to-all-done.1.msg_ref, f32[1,64,64]{2,1,0:T(8,128)S(1)} %copy-done, f32[1,64,64]{2,1,0:T(8,128)S(1)} %copy-done.1, f32[1280,128]{1,0:T(8,128)S(1)} %get-tuple-element.16.base_ref, ...), custom_call_target="tpu_custom_call" | custom-call | tf_op jit(solution)/shard_map/finish/pallas_call | solution.py:481
  58.5 16.6 %all_to_all.15.x_ref = bf16[32,4,640]{2,1,0:T(4,128)(2,1)S(1)} all-to-all(bf16[32,4,640]{2,1,0:T(4,128)(2,1)S(1)} %finish.1), channel_id=1, replica_groups=mesh['seg'=16,'grp'=32] {'grp'}, dimensions={0} | all-to-all | bytes 327680 | tf_op jit(solution)/shard_map/all_to_all | solution.py:523
  75.1 0.8 %unpack.1 = bf16[40,2048]{1,0:T(8,128)(2,1)} custom-call(bf16[32,4,640]{2,1,0:T(4,128)(2,1)S(1)} %all_to_all.15.x_ref), custom_call_target="tpu_custom_call" | custom-call | tf_op jit(solution)/shard_map/unpack/pallas_call | solution.py:513
Async XLA Ops:
  2.0 29.6 %all-to-all-start = ((bf16[32,64,128]{2,1,0:T(8,128)(2,1)}), bf16[32,64,128]{2,1,0:T(8,128)(2,1)S(1)}, u32[]{:S(2)}, u32[]{:S(2)}) async-start(bf16[32,64,128]{2,1,0:T(8,128)(2,1)} %pack.1), calls=%async_computation | async-start | bytes 1048576 | tf_op jit(solution)/shard_map/all_to_all | solution.py:523
  36.7 20.3 %all-to-all-start.1 = ((bf16[16,64,128]{2,1,0:T(8,128)(2,1)}), bf16[16,64,128]{2,1,0:T(8,128)(2,1)S(1)}, u32[]{:S(2)}, u32[]{:S(2)}) async-start(bf16[16,64,128]{2,1,0:T(8,128)(2,1)} %get-tuple-element.12), calls=%async_computation.1 | async-start | bytes 524288 | tf_op jit(solution)/shard_map/all_to_all | solution.py:523
  45.8 11.2 %copy-start = (f32[1,64,64]{2,1,0:T(8,128)S(1)}, f32[1,64,64]{2,1,0:T(8,128)}, u32[]{:S(2)}) copy-start(f32[1,64,64]{2,1,0:T(8,128)} %sf_ref.1) | copy-start | bytes 49156
  45.8 11.2 %copy-start.1 = (f32[1,64,64]{2,1,0:T(8,128)S(1)}, f32[1,64,64]{2,1,0:T(8,128)}, u32[]{:S(2)}) copy-start(f32[1,64,64]{2,1,0:T(8,128)} %sb_ref.1) | copy-start | bytes 49156
